TPU v7x, 128 devices: a whole 4x4x4 slice. The times are simulated.
128 devices in a mesh: row: 8 (over x, z_hi), col: 16 (over y, z_lo, core).
Axes of the slice: x: 4, y: 4, z: 4 (z_hi: 2, z_lo: 2; z = z_hi * 2 + z_lo), core: 2. Of those that a mesh axis runs over, the one named last changes fastest.
Arguments:
- increments: bfloat16 [2048, 8192], P('col', 'row'), may hold values from -48 to 48
- states: bfloat16 [2048, 65536], P(('row', 'col')), may hold values from -24 to 24
- group_date: int32 [128], replicated, may hold values from 0 to 127, each once
Outputs:
- covariance: float32 [8192, 65536], P('row', 'col')
Inputs may be any that keep to these rules, and one draw needn't show every extreme that they name: `group_date`: a permutation: each of the 128 date groups is named once.
All inputs are finite; a program needn't handle non-finite values.
Results may differ from a plain program's by a relative error of at most 0.0003.
Values may be sent and summed in bfloat16 or wider, within the bound.
No kernel may reach another device: no remote copies, remote signals or barrier semaphores. Data moves between devices by JAX's collectives and lax.ppermute only.
A program may use at most 128 MiB of HBM per device.

v0:
```python
import jax
import jax.numpy as jnp
from jax import lax
from jax.sharding import PartitionSpec as P


def body(increments, states, group_date):
    group_len = states.shape[0]
    inc_all = lax.all_gather(increments, "col", axis=0, tiled=True)
    dates = inc_all.shape[0]
    inc_sum = jnp.sum(inc_all.astype(jnp.float32), axis=0)
    block = lax.all_to_all(states, "col", split_axis=1, concat_axis=0, tiled=True)
    panel = lax.all_gather(block, "row", axis=0, tiled=True)
    groups = jnp.arange(dates // group_len, dtype=jnp.int32)
    starts = jnp.take(group_date, groups, axis=0) * group_len
    positions = (starts[:, None] + jnp.arange(group_len, dtype=jnp.int32)[None, :]).reshape(-1)
    rows = jnp.take(inc_all, positions, axis=0)
    cross = lax.dot_general(
        rows, panel, (((0,), (0,)), ((), ())), preferred_element_type=jnp.float32
    )
    state_sum = jnp.sum(panel.astype(jnp.float32), axis=0)
    inc_mean = inc_sum / dates
    state_mean = state_sum / dates
    correction = dates * (inc_mean[:, None] * state_mean[None, :])
    return (cross - correction) / (dates - 1)


def solution(mesh):
    in_specs = (P("col", "row"), P(("row", "col"), None), P())
    out_specs = P("row", "col")
    return jax.shard_map(body, mesh=mesh, in_specs=in_specs, out_specs=out_specs, check_vma=False)
```

profile of v0, /device:TPU:8, one launch (start us, length us, event | category | flops | bytes accessed | tf_op | source)
XLA Modules:
  0.0 296.6 jit_solution(6967212530158207782)
XLA Ops:
  6.5 0.0 copy-start
  6.5 0.0 all-gather.3.cloned.1.call-start
  6.5 0.7 all-gather.3.cloned.1.call-update
  7.3 0.0 all-gather.5.cloned.1.call-start
  7.3 1.7 copy.8
  9.0 42.8 %all_to_all.19 = bf16[16,16,4096]{2,0,1:T(8,128)(2,1)} all-to-all(bf16[16,16,4096]{2,0,1:T(8,128)(2,1)S(1)} %bitcast.10), channel_id=1, replica_groups=mesh['row'=8,'col'=16] {'col'}, dimensions={1} | all-to-all | bytes 4194304 | tf_op jit(solution)/shard_map/all_to_all | solution.py:12
  51.9 0.0 all-gather.5.cloned.1.call-update
  51.9 0.0 copy-done
  51.9 1.2 gather_fusion
  53.2 0.1 iota_add_fusion
  53.2 0.1 add.60
  53.3 0.1 add.57
  53.5 10.3 %all-gather.3.cloned.1.call-done = bf16[2048,1024]{1,0:T(8,128)(2,1)} async-done(((bf16[128,1024]{1,0:T(8,128)(2,1)}), bf16[2048,1024]{1,0:T(8,128)(2,1)}) %all-gather.3.cloned.1.call-update) | async-done | bytes 4194320 | tf_op jit(solution)/shard_map/all_gather | solution.py:9
  63.7 13.8 %gather_fusion.1 = bf16[2048,1024]{1,0:T(8,128)(2,1)} fusion(bf16[2048,1024]{1,0:T(8,128)(2,1)} %all-gather.3.cloned.1.call-done, s32[2048]{0:T(1024)S(1)} %broadcast_clamp_fusion), kind=kCustom, calls=%fused_computation.1 | custom fusion | bytes 8396800 | tf_op jit(solution)/shard_map/jit(_take)/gather | solution.py:17
  77.5 3.6 %convert_reduce_fusion.1 = f32[1024]{0:T(1024)S(1)} fusion(bf16[2048,1024]{1,0:T(8,128)(2,1)} %all-gather.3.cloned.1.call-done), kind=kLoop, calls=%fused_computation.4 | loop fusion | flops 4193280 | bytes 4198400 | tf_op jit(solution)/shard_map/reduce_sum | solution.py:11
  81.1 172.7 %all-gather.5.cloned.1.call-done = bf16[2048,4096]{1,0:T(8,128)(2,1)} async-done(((bf16[256,4096]{1,0:T(8,128)(2,1)}), bf16[2048,4096]{1,0:T(8,128)(2,1)}) %all-gather.5.cloned.1.call-update) | async-done | bytes 16777232 | tf_op jit(solution)/shard_map/all_gather | solution.py:13
  253.8 0.0 copy-start.1
  253.8 7.0 %convert_reduce_fusion = f32[4096]{0:T(1024)S(1)} fusion(bf16[2048,4096]{1,0:T(8,128)(2,1)} %all-gather.5.cloned.1.call-done), kind=kLoop, calls=%fused_computation.2 | loop fusion | flops 16773120 | bytes 16793600 | tf_op jit(solution)/shard_map/reduce_sum | solution.py:21
  260.8 3.8 %copy-done.1 = bf16[2048,4096]{1,0:T(8,128)(2,1)S(1)} copy-done((bf16[2048,4096]{1,0:T(8,128)(2,1)S(1)}, bf16[2048,4096]{1,0:T(8,128)(2,1)}, u32[]{:S(2)}) %copy-start.1) | copy-done | bytes 16777240
  264.6 25.1 %subtract_multiply_fusion = f32[1024,4096]{1,0:T(8,128)} fusion(bf16[2048,4096]{1,0:T(8,128)(2,1)S(1)} %copy-done.1, f32[4096]{0:T(1024)S(1)} %broadcast_multiply_fusion, f32[1024]{0:T(1024)S(1)} %broadcast_multiply_fusion.1, bf16[2048,1024]{1,0:T(8,128)(2,1)} %gather_fusion.1, pred[2048]{0:T(1024)(128)(4,1)S(1)} %compare_and_fusion), kind=kOutput, calls=%fused_computation.3 | convolution fusion | flops 17198743552 | bytes 37771264 | tf_op jit(solution)/shard_map/dot_general | solution.py:18
  (8 shorter events, 0.1 us)
Async XLA Ops:
  6.5 45.4 %copy-start = (s32[128]{0:T(128)S(1)}, s32[128]{0:T(128)}, u32[]{:S(2)}) copy-start(s32[128]{0:T(128)} %param.5) | copy-start | bytes 1540
  6.5 57.2 %all-gather.3.cloned.1.call-start = ((), (), s32[]{:S(2)}) async-start(), calls=%async_computation.1 | async-start | bytes 4456448 | tf_op jit(solution)/shard_map/all_gather | solution.py:9
  7.3 246.6 %all-gather.5.cloned.1.call-start = ((), (), s32[]{:S(2)}) async-start(), calls=%async_computation.2 | async-start | bytes 18874368 | tf_op jit(solution)/shard_map/all_gather | solution.py:13
  253.8 10.8 %copy-start.1 = (bf16[2048,4096]{1,0:T(8,128)(2,1)S(1)}, bf16[2048,4096]{1,0:T(8,128)(2,1)}, u32[]{:S(2)}) copy-start(bf16[2048,4096]{1,0:T(8,128)(2,1)} %all-gather.5.cloned.1.call-done) | copy-start | bytes 50331652
Sparse Core Ops, SparseCore 0:
  9.1 54.6 all-gather.2
  66.1 187.7 all-gather.4
where the time goes:
time: 297 us
  waiting for transfers between devices  184 us (62%)
  blocking collectives  42.8 us (14%)
  matrix products  25.1 us (8%)
  local copies, waits for them, and re-layouts  20.7 us (7%)
  between operations  13.5 us (5%)
  other arithmetic  10.7 us (4%)
    all_gather x1, waiting for transfers between devices, body(): panel = lax.all_gather(block, 'row', axis=0, tiled=True)  173 us
    all_to_all x1, blocking collectives, body(): lax.all_to_all(states, 'col', split_axis=1, concat_axis=0, tiled=True)  42.8 us
    dot_general x1, matrix products, body(): lax.dot_general(rows, panel, (((0,), (0,)), ((), ())), preferred_element_...  25.1 us
    gather x1, local copies, waits for them, and re-layouts, body(): rows = jnp.take(inc_all, positions, axis=0)  13.8 us
    all_gather x1, waiting for transfers between devices, body(): inc_all = lax.all_gather(increments, 'col', axis=0, tiled=True)  10.3 us
    reduce_sum x1, other arithmetic, body(): state_sum = jnp.sum(panel.astype(jnp.float32), axis=0)  6.97 us
  transfers between devices with their start and end apart: 2, of which 2 were waited for; matrix products, arithmetic and copies ran while one was open for 7% of the time, Pallas kernels for 0%

commit v1 on v0

v1 whole, which is shorter than its diff:
```python
import functools

import jax
import jax.numpy as jnp
from jax import lax
from jax.experimental import pallas as pl
from jax.experimental.pallas import tpu as pltpu
from jax.sharding import PartitionSpec as P

AXES = ("row", "col")
NX, NY, NZ, NC = 4, 4, 4, 2
NCOL = NY * 2 * NC
TILE = 512
WIDTHS = (1024, 1536, 1536)


def device(x, y, z, c):
    return ((x % NX) * 2 + (z % NZ) // 2) * NCOL + ((y % NY) * 2 + (z % NZ) % 2) * NC + c


def moves(to):
    return [
        (device(x, y, z, c), device(*to(x, y, z, c)))
        for x in range(NX) for y in range(NY) for z in range(NZ) for c in range(NC)
    ]


X_UP = moves(lambda x, y, z, c: (x + 1, y, z, c))
X_DOWN = moves(lambda x, y, z, c: (x - 1, y, z, c))
X_FAR = moves(lambda x, y, z, c: (x + 2, y, z, c))
SAME_X = [[x * 2 * NCOL + i for i in range(2 * NCOL)] for x in range(NX)]
ALONG_X = [[2 * x + h for x in range(NX)] for h in range(2)]


def align_kernel(starts, inc_ref, out_ref, sum_ref, held, sem):
    dates, comps = held.shape
    group = dates // starts.shape[0]

    def send(i, carry):
        source = pl.multiple_of(starts[i], group)
        target = pl.multiple_of(i * group, group)
        pltpu.make_async_copy(
            inc_ref.at[pl.ds(source, group)], held.at[pl.ds(target, group)], sem
        ).start()
        return carry

    lax.fori_loop(0, starts.shape[0], send, 0)
    pltpu.make_async_copy(inc_ref, held, sem).wait()
    step = 256
    total = jnp.zeros((comps, 1), jnp.float32)
    for i in range(dates // step):
        turned = held[i * step:(i + 1) * step, :].T
        out_ref[:, i * step:(i + 1) * step] = turned
        total = total + jnp.sum(turned.astype(jnp.float32), axis=1, keepdims=True)
    sum_ref[...] = total


def align(starts, inc_all):
    dates, comps = inc_all.shape
    return pl.pallas_call(
        align_kernel,
        out_shape=(
            jax.ShapeDtypeStruct((comps, dates), inc_all.dtype),
            jax.ShapeDtypeStruct((comps, 1), jnp.float32),
        ),
        in_specs=[
            pl.BlockSpec(memory_space=pltpu.SMEM),
            pl.BlockSpec(memory_space=pl.ANY),
        ],
        out_specs=(
            pl.BlockSpec(memory_space=pltpu.VMEM),
            pl.BlockSpec(memory_space=pltpu.VMEM),
        ),
        scratch_shapes=[pltpu.VMEM((dates, comps), inc_all.dtype), pltpu.SemaphoreType.DMA],
        compiler_params=pltpu.CompilerParams(vmem_limit_bytes=60 * 2**20),
        cost_estimate=pl.CostEstimate(flops=comps, bytes_accessed=comps, transcendentals=0),
        name="align",
    )(starts, inc_all)


def gather_panel(places, panels):
    return [(0, panels[0][...])]


def exchange_panel(places, panels):
    sources, nx, group, width = panels[0].shape
    depth = sources * group
    return [
        (pl.multiple_of(places[i], depth), panels[0][:, i].reshape(depth, width))
        for i in range(nx)
    ]


def ring_panel(places, panels):
    order = (0, 1, 3, 2, 4)
    return [
        (pl.multiple_of(places[i], panel.shape[0]), panel[...]) for i, panel in zip(order, panels)
    ]


def product_kernel(pieces, places, rows_ref, sum_ref, *refs):
    dates = rows_ref.shape[1]
    panels, out_ref = refs[:-1], refs[-1]
    acc, state_sum = None, None
    for place, piece in pieces(places, panels):
        part = jnp.dot(
            rows_ref[:, pl.ds(place, piece.shape[0])], piece, preferred_element_type=jnp.float32
        )
        partial_sum = jnp.sum(piece.astype(jnp.float32), axis=0, keepdims=True)
        acc = part if acc is None else acc + part
        state_sum = partial_sum if state_sum is None else state_sum + partial_sum
    inc_mean = sum_ref[...] / dates
    state_mean = state_sum / dates
    out_ref[...] = (acc - dates * (inc_mean * state_mean)) * (1.0 / (dates - 1))


def product(pieces, places, rows, inc_sum, panels, offset, columns, out):
    comps, dates = rows.shape
    width = panels[0].shape[-1]
    base = offset // TILE
    whole = pl.Buffered(1)
    in_specs = [
        pl.BlockSpec(memory_space=pltpu.SMEM),
        pl.BlockSpec(rows.shape, lambda j: (0, 0), pipeline_mode=whole),
        pl.BlockSpec(inc_sum.shape, lambda j: (0, 0), pipeline_mode=whole),
    ]
    for panel in panels:
        lead = (0,) * (panel.ndim - 1)
        in_specs.append(pl.BlockSpec(panel.shape[:-1] + (TILE,), lambda j, lead=lead: lead + (j,)))
    args = [places, rows, inc_sum] + panels
    aliases = {}
    kernel = functools.partial(product_kernel, pieces)
    if out is not None:
        in_specs.append(pl.BlockSpec(memory_space=pl.ANY))
        aliases = {len(args): 0}
        args.append(out)

        def kernel(*refs):
            product_kernel(pieces, *refs[:-2], refs[-1])

    return pl.pallas_call(
        kernel,
        out_shape=jax.ShapeDtypeStruct((comps, columns), jnp.float32),
        grid=(width // TILE,),
        in_specs=in_specs,
        out_specs=pl.BlockSpec((comps, TILE), lambda j: (0, base + j)),
        input_output_aliases=aliases,
        compiler_params=pltpu.CompilerParams(vmem_limit_bytes=60 * 2**20),
        cost_estimate=pl.CostEstimate(flops=comps, bytes_accessed=comps, transcendentals=0),
        name="product",
    )(*args)


def body(increments, states, group_date):
    group, total = states.shape
    columns = total // NCOL
    dates = group * group_date.shape[0]
    blocks = states.reshape(group, NCOL, columns)
    barrier = lax.optimization_barrier

    def part(offset, width):
        return blocks[:, :, offset:offset + width].transpose(1, 0, 2)

    def spread(got):
        return lax.all_gather(got, "row", axis=0, tiled=True, axis_index_groups=ALONG_X)

    def exchange(sent):
        both = jnp.broadcast_to(sent[None], (2,) + sent.shape).reshape((-1,) + sent.shape[1:])
        return lax.all_to_all(both, AXES, 0, 0, tiled=True, axis_index_groups=SAME_X)

    wa, wb, wc = WIDTHS
    x = lax.axis_index("row") // 2
    depth = dates // NX
    places = jnp.stack(
        [(x + step) % NX * depth for step in range(NX)] + [(x + 2) % NX * depth + depth // 2]
    ).astype(jnp.int32)

    inc_all = lax.all_gather(increments, "col", axis=0, tiled=True)
    raw = part(0, wa)
    raw_left = lax.ppermute(raw, AXES, X_UP)
    raw_right = lax.ppermute(raw, AXES, X_DOWN)
    raw_far = lax.ppermute(raw, AXES, X_FAR)
    gotc = exchange(part(wa + wb, wc)).reshape(-1, wc)

    sentb, raw, raw_left, raw_right, raw_far, gotc = barrier(
        (part(wa, wb), raw, raw_left, raw_right, raw_far, gotc)
    )
    left = lax.ppermute(gotc, AXES, X_UP)
    right = lax.ppermute(gotc, AXES, X_DOWN)
    gotb = exchange(sentb).reshape(-1, wb)

    raw, raw_left, raw_right, raw_far, gotc, left, right, gotb = barrier(
        (raw, raw_left, raw_right, raw_far, gotc, left, right, gotb)
    )
    panelb = spread(gotb)
    far_left = lax.ppermute(left[:depth // 2], AXES, X_UP)
    far_right = lax.ppermute(right[depth // 2:], AXES, X_DOWN)
    raw = jnp.stack([raw, raw_right, raw_far, raw_left], axis=1)
    gota = exchange(raw.reshape(NCOL, NX * group, wa)).reshape(2 * NCOL, NX, group, wa)
    rows, inc_sum = align(group_date * group, inc_all)
    ring = [gotc, right, left, far_left, far_right]
    out = product(ring_panel, places, rows, inc_sum, ring, wa + wb, columns, None)

    gota, out = barrier((gota, out))
    out = product(exchange_panel, places, rows, inc_sum, [gota], 0, columns, out)
    return product(gather_panel, places, rows, inc_sum, [panelb], wa, columns, out)


def solution(mesh):
    in_specs = (P("col", "row"), P(("row", "col"), None), P())
    out_specs = P("row", "col")
    return jax.shard_map(body, mesh=mesh, in_specs=in_specs, out_specs=out_specs, check_vma=False)
```

time: 297 us -> 192 us (0.65)
  waiting for transfers between devices: 184 us -> 64.4 us
  Pallas kernels: 0 us -> 39.1 us
  starting transfers between devices: 0.04 us -> 27.1 us
  matrix products: 25.1 us -> 0 us
  blocking collectives: 42.8 us -> 28.8 us
  other arithmetic: 10.7 us -> 3.49 us
  local copies, waits for them, and re-layouts: 20.7 us -> 14.5 us
    all_gather x1, waiting for transfers between devices: 173 us -> 2.06 us  [spread(): lax.all_gather(got, 'row', axis=0, tiled=True, axis_index_groups=ALONG_X)]
    ppermute x0 -> x7, waiting for transfers between devices: none -> 52.6 us  [the longest x1 27.3 us: body(): far_left = lax.ppermute(left[:depth // 2], AXES, X_UP)]
    pallas_call x0 -> x4, Pallas kernels: none -> 39.1 us  [the longest x3 32.8 us: product(): pl.pallas_call(kernel, out_shape=jax.ShapeDtypeStruct((comps, columns), j...]
    dot_general x1 -> x0, matrix products: 25.1 us -> none  [body(): lax.dot_general(rows, panel, (((0,), (0,)), ((), ())), preferred_element_...]
    all_to_all x0 -> x2, starting transfers between devices: none -> 15.2 us  [exchange(): lax.all_to_all(both, AXES, 0, 0, tiled=True, axis_index_groups=SAME_X)]
    gather x2 -> x0, local copies, waits for them, and re-layouts: 15 us -> none  [the longest x1 13.8 us: body(): rows = jnp.take(inc_all, positions, axis=0)]
    all_to_all x1, blocking collectives: 42.8 us -> 28.8 us  [exchange(): lax.all_to_all(both, AXES, 0, 0, tiled=True, axis_index_groups=SAME_X)]
    ppermute x0 -> x7, starting transfers between devices: none -> 11.8 us  [the longest x1 2.59 us: body(): far_right = lax.ppermute(right[depth // 2:], AXES, X_DOWN)]
  transfers between devices with their start and end apart: 2 -> 11, of which waited for: 2 -> 8; matrix products, arithmetic and copies ran while one was open for 7% -> 8% of each run, Pallas kernels for 0% -> 14%
where the time goes in v1:
time: 192 us; the launch traced here: 191 us
  waiting for transfers between devices  64.4 us (34%)
  Pallas kernels  39.1 us (20%)
  blocking collectives  28.8 us (15%)
  starting transfers between devices  27.1 us (14%)
  local copies, waits for them, and re-layouts  14.5 us (8%)
  between operations  13.5 us (7%)
  other arithmetic  3.49 us (2%)
    pallas_call x3, Pallas kernels, product(): pl.pallas_call(kernel, out_shape=jax.ShapeDtypeStruct((comps, columns), j...  32.8 us
    all_to_all x1, blocking collectives, exchange(): lax.all_to_all(both, AXES, 0, 0, tiled=True, axis_index_groups=SAME_X)  28.8 us
    ppermute x1, waiting for transfers between devices, body(): far_left = lax.ppermute(left[:depth // 2], AXES, X_UP)  27.3 us
    all_to_all x2, starting transfers between devices, exchange(): lax.all_to_all(both, AXES, 0, 0, tiled=True, axis_index_groups=SAME_X)  15.2 us
    ppermute x1, waiting for transfers between devices, body(): raw_right = lax.ppermute(raw, AXES, X_DOWN)  10.5 us
    ppermute x1, waiting for transfers between devices, body(): raw_left = lax.ppermute(raw, AXES, X_UP)  10.1 us
    all_to_all x2, waiting for transfers between devices, exchange(): lax.all_to_all(both, AXES, 0, 0, tiled=True, axis_index_groups=SAME_X)  8.94 us
    pallas_call x1, Pallas kernels, align(): pl.pallas_call(align_kernel, out_shape=(jax.ShapeDtypeStruct((comps, date...  6.35 us
  transfers between devices with their start and end apart: 11, of which 8 were waited for; matrix products, arithmetic and copies ran while one was open for 8% of the time, Pallas kernels for 14%

profile of v1, /device:TPU:8, one launch (start us, length us, event | category | flops | bytes accessed | tf_op | source)
XLA Modules:
  0.0 190.9 jit_solution(11917645380065869048)
XLA Ops:
  6.5 0.0 all-gather.3.cloned.1.call-start
  6.5 0.7 all-gather.3.cloned.1.call-update
  7.3 2.7 %copy.9 = bf16[2,8,16,4096]{3,2,1,0:T(8,128)(2,1)S(1)} copy(bf16[2,8,16,4096]{3,1,2,0:T(8,128)(2,1)} %bitcast.31) | data formatting | bytes 4194304
  10.0 1.0 slice_bitcast_fusion
  11.0 0.4 copy.6
  11.5 1.3 broadcast_in_dim.8
  12.8 8.6 %all-to-all-start = ((bf16[32,16,1536]{2,1,0:T(8,128)(2,1)}), bf16[32,16,1536]{2,1,0:T(8,128)(2,1)}, u32[]{:S(2)}, u32[]{:S(2)}) async-start(bf16[32,16,1536]{2,1,0:T(8,128)(2,1)} %bitcast.29), calls=%async_computation | async-start | bytes 3145728 | tf_op jit(solution)/shard_map/all_to_all | solution.py:169
  21.4 0.0 all-gather.5.cloned.1.call-start
  21.5 0.0 copy-start.2
  21.5 1.6 collective-permute-start
  23.1 1.7 collective-permute-start.1
  24.8 0.0 copy-done.2
  24.8 1.8 collective-permute-start.2
  26.6 10.1 %collective-permute-done = bf16[16,16,1024]{2,0,1:T(8,128)(2,1)S(1)} collective-permute-done((bf16[16,16,1024]{2,0,1:T(8,128)(2,1)S(1)}, bf16[16,16,1024]{2,0,1:T(8,128)(2,1)S(1)}, u32[]{:S(2)}, u32[]{:S(2)}) %collective-permute-start) | collective-permute-done | bytes 524320 | tf_op jit(solution)/shard_map/ppermute | solution.py:180
  36.8 10.5 %collective-permute-done.1 = bf16[16,16,1024]{2,0,1:T(8,128)(2,1)S(1)} collective-permute-done((bf16[16,16,1024]{2,0,1:T(8,128)(2,1)S(1)}, bf16[16,16,1024]{2,0,1:T(8,128)(2,1)S(1)}, u32[]{:S(2)}, u32[]{:S(2)}) %collective-permute-start.1) | collective-permute-done | bytes 524320 | tf_op jit(solution)/shard_map/ppermute | solution.py:181
  47.3 0.0 copy-done.5
  47.3 0.8 copy-done.6
  48.1 1.0 collective-permute-done.2
  49.1 3.0 %all-to-all-done = bf16[32,16,1536]{2,1,0:T(8,128)(2,1)} async-done(((bf16[32,16,1536]{2,1,0:T(8,128)(2,1)}), bf16[32,16,1536]{2,1,0:T(8,128)(2,1)}, u32[]{:S(2)}, u32[]{:S(2)}) %all-to-all-start) | async-done | bytes 1572896 | tf_op jit(solution)/shard_map/all_to_all | solution.py:169
  52.1 1.6 collective-permute-start.3
  53.6 1.7 collective-permute-start.4
  55.3 1.6 copy.7
  56.9 0.2 broadcast_in_dim.9
  57.1 28.8 %all_to_all.15 = bf16[32,16,1536]{2,1,0:T(8,128)(2,1)} all-to-all(bf16[32,16,1536]{2,1,0:T(8,128)(2,1)S(1)} %bitcast.30), channel_id=1, replica_groups={{0,1,2,3,4,5,6,7,8,9,10,11,12,13,14,15,16,17,18,19,20,21,22,23,24,25,26..., dimensions={0} | all-to-all | bytes 3145728 | tf_op jit(solution)/shard_map/all_to_all | solution.py:169
  85.9 3.7 %collective-permute-done.3.refs_2_ = bf16[512,1536]{1,0:T(8,128)(2,1)S(1)} collective-permute-done((bf16[512,1536]{1,0:T(8,128)(2,1)}, bf16[512,1536]{1,0:T(8,128)(2,1)S(1)}, u32[]{:S(2)}, u32[]{:S(2)}) %collective-permute-start.3) | collective-permute-done | bytes 1572896 | tf_op jit(solution)/shard_map/ppermute | solution.py:188
  89.6 0.0 collective-permute-done.4.refs_1_
  89.6 0.0 all-gather.5.cloned.1.call-update
  89.6 2.9 %pad_maximum_fusion = bf16[16,4,16,1024]{3,0,2,1:T(8,128)(2,1)S(1)} fusion(bf16[16,1,16,1024]{3,0,2,1:T(8,128)(2,1)} %bitcast.33, bf16[16,1,16,1024]{3,0,2,1:T(8,128)(2,1)} %bitcast.14, bf16[16,1,16,1024]{3,0,2,1:T(8,128)(2,1)} %bitcast.34, bf16[16,1,16,1024]{3,0,2,1:T(8,128)(2,1)} %bitcast.32), kind=kLoop, calls=%fused_computation | loop fusion | flops 3145728 | bytes 4194304 | tf_op jit(solution)/shard_map/stack | solution.py:198
  92.5 1.2 copy.8
  93.7 2.5 %broadcast_in_dim.22 = bf16[2,16,64,1024]{3,2,1,0:T(8,128)(2,1)} broadcast(bf16[16,64,1024]{2,1,0:T(8,128)(2,1)S(1)} %copy.8), dimensions={1,2,3} | broadcast | bytes 6291456 | tf_op jit(solution)/shard_map/broadcast_in_dim | solution.py:168
  96.2 6.6 %all-to-all-start.2 = ((bf16[32,64,1024]{2,1,0:T(8,128)(2,1)}), bf16[32,64,1024]{2,1,0:T(8,128)(2,1)}, u32[]{:S(2)}, u32[]{:S(2)}) async-start(bf16[32,64,1024]{2,1,0:T(8,128)(2,1)} %bitcast.24), calls=%async_computation.2 | async-start | bytes 8388608 | tf_op jit(solution)/shard_map/all_to_all | solution.py:169
  102.8 0.0 copy-start.7
  102.8 0.9 slice.18
  103.8 0.9 collective-permute-start.5
  104.7 0.1 slice.19
  104.7 2.6 %collective-permute-start.6 = (bf16[256,1536]{1,0:T(8,128)(2,1)S(1)}, bf16[256,1536]{1,0:T(8,128)(2,1)S(1)}, u32[]{:S(2)}, u32[]{:S(2)}) collective-permute-start(bf16[256,1536]{1,0:T(8,128)(2,1)S(1)} %slice.19), channel_id=1, source_target_pairs={{0,96},{1,97},{2,98},{3,99},{16,112},{17,113},{18,114},{19,115},{4... | collective-permute-start | bytes 2359304 | tf_op jit(solution)/shard_map/ppermute | solution.py:197
  107.3 0.6 stack.38.places.refs_0_
  107.9 0.6 broadcast_multiply_fusion.starts
  108.5 6.4 %align.1 = (bf16[1024,2048]{1,0:T(8,128)(2,1)}, f32[1024,1]{1,0:T(8,128)}) custom-call(s32[128]{0:T(128)} %broadcast_multiply_fusion.starts, bf16[2048,1024]{1,0:T(8,128)(2,1)} %all-gather.3.cloned.1.call-done.inc_ref), custom_call_target="tpu_custom_call" | custom-call | flops 1024 | bytes 1024 | tf_op jit(solution)/shard_map/align/pallas_call | solution.py:60
  114.9 27.3 %collective-permute-done.5.refs_3_ = bf16[256,1536]{1,0:T(8,128)(2,1)S(1)} collective-permute-done((bf16[256,1536]{1,0:T(8,128)(2,1)}, bf16[256,1536]{1,0:T(8,128)(2,1)S(1)}, u32[]{:S(2)}, u32[]{:S(2)}) %collective-permute-start.5) | collective-permute-done | bytes 786464 | tf_op jit(solution)/shard_map/ppermute | solution.py:196
  142.2 0.0 collective-permute-done.6.refs_4_
  142.2 0.9 copy-done.3
  143.0 0.3 copy-done.4
  143.3 12.1 %product.3.refs_4_ = f32[1024,4096]{1,0:T(8,128)} custom-call(s32[5]{0:T(128)} %stack.38.places.refs_0_, bf16[1024,2048]{1,0:T(8,128)(2,1)} %get-tuple-element.23.rows_ref.refs_1_, f32[1024,1]{1,0:T(8,128)} %get-tuple-element.24.sum_ref.refs_2_, bf16[512,1536]{1,0:T(8,128)(2,1)} %bitcast.9.refs_0_, bf16[512,1536]{1,0:T(8,128)(2,1)} %copy-done.1, ...), custom_call_target="tpu_custom_call" | custom-call | flops 1024 | bytes 1024 | tf_op jit(solution)/shard_map/product/pallas_call | solution.py:141
  155.4 6.0 %all-to-all-done.2 = bf16[32,64,1024]{2,1,0:T(8,128)(2,1)} async-done(((bf16[32,64,1024]{2,1,0:T(8,128)(2,1)}), bf16[32,64,1024]{2,1,0:T(8,128)(2,1)}, u32[]{:S(2)}, u32[]{:S(2)}) %all-to-all-start.2) | async-done | bytes 4194336 | tf_op jit(solution)/shard_map/all_to_all | solution.py:169
  161.4 9.1 %product.4.refs_4_ = f32[1024,4096]{1,0:T(8,128)} custom-call(s32[5]{0:T(128)} %stack.38.places.refs_0_, bf16[1024,2048]{1,0:T(8,128)(2,1)} %get-tuple-element.23.rows_ref.refs_1_, f32[1024,1]{1,0:T(8,128)} %get-tuple-element.24.sum_ref.refs_2_, bf16[32,4,16,1024]{3,2,1,0:T(8,128)(2,1)} %bitcast.18.refs_3_, ...), custom_call_target="tpu_custom_call", output_to_operand_aliasing={{}: (4, {})} | custom-call | flops 1024 | bytes 1024 | tf_op jit(solution)/shard_map/product/pallas_call | solution.py:141
  170.5 2.1 %all-gather.5.cloned.1.call-done.refs_3_ = bf16[2048,1536]{1,0:T(8,128)(2,1)} async-done(((bf16[512,1536]{1,0:T(8,128)(2,1)}), bf16[2048,1536]{1,0:T(8,128)(2,1)}) %all-gather.5.cloned.1.call-update) | async-done | bytes 6291472 | tf_op jit(solution)/shard_map/all_gather | solution.py:165
  172.6 11.5 %product.5 = f32[1024,4096]{1,0:T(8,128)} custom-call(s32[5]{0:T(128)} %stack.38.places.refs_0_, bf16[1024,2048]{1,0:T(8,128)(2,1)} %get-tuple-element.23.rows_ref.refs_1_, f32[1024,1]{1,0:T(8,128)} %get-tuple-element.24.sum_ref.refs_2_, bf16[2048,1536]{1,0:T(8,128)(2,1)} %all-gather.5.cloned.1.call-done.refs_3_, ...), custom_call_target="tpu_custom_call", output_to_operand_aliasing={{}: (4, {})} | custom-call | flops 1024 | bytes 1024 | tf_op jit(solution)/shard_map/product/pallas_call | solution.py:141
  (11 shorter events, 0.1 us)
Async XLA Ops:
  6.5 102.0 %all-gather.3.cloned.1.call-start = ((), (), s32[]{:S(2)}) async-start(), calls=%async_computation.3 | async-start | bytes 4456448 | tf_op jit(solution)/shard_map/all_gather | solution.py:178
  12.8 39.3 %all-to-all-start = ((bf16[32,16,1536]{2,1,0:T(8,128)(2,1)}), bf16[32,16,1536]{2,1,0:T(8,128)(2,1)}, u32[]{:S(2)}, u32[]{:S(2)}) async-start(bf16[32,16,1536]{2,1,0:T(8,128)(2,1)} %bitcast.29), calls=%async_computation | async-start | bytes 3145728 | tf_op jit(solution)/shard_map/all_to_all | solution.py:169
  21.4 151.2 %all-gather.5.cloned.1.call-start = ((), (), s32[]{:S(2)}) async-start(), calls=%async_computation.4 | async-start | bytes 7864320 | tf_op jit(solution)/shard_map/all_gather | solution.py:165
  21.5 3.3 %copy-start.2 = (bf16[16,16,1024]{2,0,1:T(8,128)(2,1)}, bf16[16,16,1024]{2,0,1:T(8,128)(2,1)S(1)}, u32[]{:S(2)}) copy-start(bf16[16,16,1024]{2,0,1:T(8,128)(2,1)S(1)} %slice_bitcast_fusion.2) | copy-start | bytes 1572868
  21.5 15.3 %collective-permute-start = (bf16[16,16,1024]{2,0,1:T(8,128)(2,1)S(1)}, bf16[16,16,1024]{2,0,1:T(8,128)(2,1)S(1)}, u32[]{:S(2)}, u32[]{:S(2)}) collective-permute-start(bf16[16,16,1024]{2,0,1:T(8,128)(2,1)S(1)} %slice_bitcast_fusion.2), channel_id=1, source_target_pairs={{0,32},{1,33},{2,34},{3,35},{16,48},{17,49},{18,50},{19,51},{4,36}... | collective-permute-start | bytes 1572872 | tf_op jit(solution)/shard_map/ppermute | solution.py:180
  23.1 24.2 %collective-permute-start.1 = (bf16[16,16,1024]{2,0,1:T(8,128)(2,1)S(1)}, bf16[16,16,1024]{2,0,1:T(8,128)(2,1)S(1)}, u32[]{:S(2)}, u32[]{:S(2)}) collective-permute-start(bf16[16,16,1024]{2,0,1:T(8,128)(2,1)S(1)} %slice_bitcast_fusion.2), channel_id=1, source_target_pairs={{0,96},{1,97},{2,98},{3,99},{16,112},{17,113},{18,114},{19,115},{4... | collective-permute-start | bytes 1572872 | tf_op jit(solution)/shard_map/ppermute | solution.py:181
  24.8 24.3 %collective-permute-start.2 = (bf16[16,16,1024]{2,0,1:T(8,128)(2,1)S(1)}, bf16[16,16,1024]{2,0,1:T(8,128)(2,1)}, u32[]{:S(2)}, u32[]{:S(2)}) collective-permute-start(bf16[16,16,1024]{2,0,1:T(8,128)(2,1)S(1)} %slice_bitcast_fusion.2), channel_id=1, source_target_pairs={{0,64},{1,65},{2,66},{3,67},{16,80},{17,81},{18,82},{19,83},{4,68}... | collective-permute-start | bytes 1572872 | tf_op jit(solution)/shard_map/ppermute | solution.py:182
  36.8 10.5 %copy-start.5 = (bf16[16,16,1024]{2,0,1:T(8,128)(2,1)}, bf16[16,16,1024]{2,0,1:T(8,128)(2,1)S(1)}, u32[]{:S(2)}) copy-start(bf16[16,16,1024]{2,0,1:T(8,128)(2,1)S(1)} %collective-permute-done) | copy-start | bytes 1572868
  47.3 0.8 copy-start.6
  52.1 37.5 %collective-permute-start.3 = (bf16[512,1536]{1,0:T(8,128)(2,1)}, bf16[512,1536]{1,0:T(8,128)(2,1)S(1)}, u32[]{:S(2)}, u32[]{:S(2)}) collective-permute-start(bf16[512,1536]{1,0:T(8,128)(2,1)} %bitcast.9.refs_0_), channel_id=1, source_target_pairs={{0,32},{1,33},{2,34},{3,35},{16,48},{17,49},{18,50},{19,51},{4,36}... | collective-permute-start | bytes 4718600 | tf_op jit(solution)/shard_map/ppermute | solution.py:188
  53.6 36.0 %collective-permute-start.4 = (bf16[512,1536]{1,0:T(8,128)(2,1)}, bf16[512,1536]{1,0:T(8,128)(2,1)S(1)}, u32[]{:S(2)}, u32[]{:S(2)}) collective-permute-start(bf16[512,1536]{1,0:T(8,128)(2,1)} %bitcast.9.refs_0_), channel_id=1, source_target_pairs={{0,96},{1,97},{2,98},{3,99},{16,112},{17,113},{18,114},{19,115},{4... | collective-permute-start | bytes 4718600 | tf_op jit(solution)/shard_map/ppermute | solution.py:189
  89.6 13.2 %copy-start = (bf16[512,1536]{1,0:T(8,128)(2,1)}, bf16[512,1536]{1,0:T(8,128)(2,1)S(1)}, u32[]{:S(2)}) copy-start(bf16[512,1536]{1,0:T(8,128)(2,1)S(1)} %collective-permute-done.3.refs_2_) | copy-start | bytes 4718596
  89.6 15.1 %copy-start.1 = (bf16[512,1536]{1,0:T(8,128)(2,1)}, bf16[512,1536]{1,0:T(8,128)(2,1)S(1)}, u32[]{:S(2)}) copy-start(bf16[512,1536]{1,0:T(8,128)(2,1)S(1)} %collective-permute-done.4.refs_1_) | copy-start | bytes 4718596
  96.2 65.2 %all-to-all-start.2 = ((bf16[32,64,1024]{2,1,0:T(8,128)(2,1)}), bf16[32,64,1024]{2,1,0:T(8,128)(2,1)}, u32[]{:S(2)}, u32[]{:S(2)}) async-start(bf16[32,64,1024]{2,1,0:T(8,128)(2,1)} %bitcast.24), calls=%async_computation.2 | async-start | bytes 8388608 | tf_op jit(solution)/shard_map/all_to_all | solution.py:169
  102.8 5.1 %copy-start.7 = (s32[128]{0:T(128)S(1)}, s32[128]{0:T(128)}, u32[]{:S(2)}) copy-start(s32[128]{0:T(128)} %param.5) | copy-start | bytes 1540
  103.8 38.4 %collective-permute-start.5 = (bf16[256,1536]{1,0:T(8,128)(2,1)}, bf16[256,1536]{1,0:T(8,128)(2,1)S(1)}, u32[]{:S(2)}, u32[]{:S(2)}) collective-permute-start(bf16[256,1536]{1,0:T(8,128)(2,1)} %slice.18), channel_id=1, source_target_pairs={{0,32},{1,33},{2,34},{3,35},{16,48},{17,49},{18,50},{19,51},{4,36}... | collective-permute-start | bytes 2359304 | tf_op jit(solution)/shard_map/ppermute | solution.py:196
  104.7 37.4 %collective-permute-start.6 = (bf16[256,1536]{1,0:T(8,128)(2,1)S(1)}, bf16[256,1536]{1,0:T(8,128)(2,1)S(1)}, u32[]{:S(2)}, u32[]{:S(2)}) collective-permute-start(bf16[256,1536]{1,0:T(8,128)(2,1)S(1)} %slice.19), channel_id=1, source_target_pairs={{0,96},{1,97},{2,98},{3,99},{16,112},{17,113},{18,114},{19,115},{4... | collective-permute-start | bytes 2359304 | tf_op jit(solution)/shard_map/ppermute | solution.py:197
  142.2 0.9 copy-start.3
  142.2 1.1 copy-start.4
Sparse Core Ops, SparseCore 0:
  9.1 53.8 all-gather.2
  89.8 82.7 all-gather.4

commit v2 on v1

v2 whole, which is shorter than its diff:
```python
import functools

import jax
import jax.numpy as jnp
from jax import lax
from jax.experimental import pallas as pl
from jax.experimental.pallas import tpu as pltpu
from jax.sharding import PartitionSpec as P

AXES = ("row", "col")
NX, NY, NZ, NC = 4, 4, 4, 2
NCOL = NY * 2 * NC
TILE = 512
BLOCK = 256
WEIGHT = 8
WIDTHS = (1024, 1536, 1536)


def device(x, y, z, c):
    return ((x % NX) * 2 + (z % NZ) // 2) * NCOL + ((y % NY) * 2 + (z % NZ) % 2) * NC + c


def moves(to):
    return [
        (device(x, y, z, c), device(*to(x, y, z, c)))
        for x in range(NX) for y in range(NY) for z in range(NZ) for c in range(NC)
    ]


X_UP = moves(lambda x, y, z, c: (x + 1, y, z, c))
X_DOWN = moves(lambda x, y, z, c: (x - 1, y, z, c))
X_FAR = moves(lambda x, y, z, c: (x + 2, y, z, c))
Y_UP = moves(lambda x, y, z, c: (x, y + 1, z, c))
Y_DOWN = moves(lambda x, y, z, c: (x, y - 1, z, c))
Y_FAR = moves(lambda x, y, z, c: (x, y + 2, z, c))
Z_PAIR = moves(lambda x, y, z, c: (x, y, z ^ 1, c))
CORE = moves(lambda x, y, z, c: (x, y, z, 1 - c))
SAME_X = [[x * 2 * NCOL + i for i in range(2 * NCOL)] for x in range(NX)]


def copy_all(copies, sems):
    started = [pltpu.make_async_copy(a, b, sems.at[i]) for i, (a, b) in enumerate(copies)]
    for copy in started:
        copy.start()
    for copy in started:
        copy.wait()


def repeat(held, out_ref, sems):
    targets = held.shape[0]
    times = out_ref.shape[0] // targets
    copy_all([(held, out_ref.at[pl.ds(i * targets, targets)]) for i in range(times)], sems)


def pick_kernel(offset, states_ref, out_ref, held, sems):
    targets, _, width = held.shape
    columns = states_ref.shape[1] // targets
    copy_all(
        [
            (states_ref.at[:, pl.ds(t * columns + offset, width)], held.at[t])
            for t in range(targets)
        ],
        sems,
    )
    repeat(held, out_ref, sems)


def pick(states, offset, width, times):
    shape = (NCOL, states.shape[0], width)
    return pl.pallas_call(
        functools.partial(pick_kernel, offset),
        out_shape=jax.ShapeDtypeStruct((times * NCOL,) + shape[1:], states.dtype),
        in_specs=[pl.BlockSpec(memory_space=pl.ANY)],
        out_specs=pl.BlockSpec(memory_space=pl.ANY),
        scratch_shapes=[pltpu.VMEM(shape, states.dtype), pltpu.SemaphoreType.DMA((NCOL,))],
        compiler_params=pltpu.CompilerParams(vmem_limit_bytes=60 * 2**20),
        cost_estimate=pl.CostEstimate(flops=width, bytes_accessed=width, transcendentals=0),
        name="pick",
    )(states)


def join_kernel(*refs):
    parts, out_ref, held, sems = refs[:-3], refs[-3], refs[-2], refs[-1]
    copy_all([(part, held.at[:, i]) for i, part in enumerate(parts)], sems)
    repeat(held, out_ref, sems)


def join(parts):
    targets, group, width = parts[0].shape
    shape = (targets, len(parts), group, width)
    return pl.pallas_call(
        join_kernel,
        out_shape=jax.ShapeDtypeStruct((2 * targets,) + shape[1:], parts[0].dtype),
        in_specs=[pl.BlockSpec(memory_space=pl.ANY)] * len(parts),
        out_specs=pl.BlockSpec(memory_space=pl.ANY),
        scratch_shapes=[
            pltpu.VMEM(shape, parts[0].dtype),
            pltpu.SemaphoreType.DMA((len(parts),)),
        ],
        compiler_params=pltpu.CompilerParams(vmem_limit_bytes=60 * 2**20),
        cost_estimate=pl.CostEstimate(flops=width, bytes_accessed=width, transcendentals=0),
        name="join",
    )(*parts)


def align_kernel(starts, mine_ref, other_ref, out_ref, sum_ref, held, sem):
    dates, comps = held.shape
    group = dates // starts.shape[0]
    half = dates // 2

    def send(i, carry):
        start = starts[i]
        target = held.at[pl.ds(pl.multiple_of(i * group, group), group)]

        @pl.when(start < half)
        def _():
            source = mine_ref.at[pl.ds(pl.multiple_of(start, group), group)]
            pltpu.make_async_copy(source, target, sem).start()

        @pl.when(start >= half)
        def _():
            source = other_ref.at[pl.ds(pl.multiple_of(start - half, group), group)]
            pltpu.make_async_copy(source, target, sem).start()

        return carry

    lax.fori_loop(0, starts.shape[0], send, 0)
    pltpu.make_async_copy(held, held, sem).wait()
    step = 256
    total = jnp.zeros((comps, 1), jnp.float32)
    for i in range(dates // step):
        turned = held[i * step:(i + 1) * step, :].T
        out_ref[:, i * step:(i + 1) * step] = turned
        total = total + jnp.sum(turned.astype(jnp.float32), axis=1, keepdims=True)
    sum_ref[...] = total


def align(starts, mine, other):
    dates, comps = 2 * mine.shape[0], mine.shape[1]
    return pl.pallas_call(
        align_kernel,
        out_shape=(
            jax.ShapeDtypeStruct((comps, dates), mine.dtype),
            jax.ShapeDtypeStruct((comps, 1), jnp.float32),
        ),
        in_specs=[
            pl.BlockSpec(memory_space=pltpu.SMEM),
            pl.BlockSpec(memory_space=pl.ANY),
            pl.BlockSpec(memory_space=pl.ANY),
        ],
        out_specs=(
            pl.BlockSpec(memory_space=pltpu.VMEM),
            pl.BlockSpec(memory_space=pltpu.VMEM),
        ),
        scratch_shapes=[pltpu.VMEM((dates, comps), mine.dtype), pltpu.SemaphoreType.DMA],
        compiler_params=pltpu.CompilerParams(vmem_limit_bytes=60 * 2**20),
        cost_estimate=pl.CostEstimate(flops=comps, bytes_accessed=comps, transcendentals=0),
        name="align",
    )(starts, mine, other)


def exchange_panel(places, panels):
    sources, nx, group, width = panels[0].shape
    depth = sources * group
    return [
        (pl.multiple_of(places[i], depth), panels[0][:, i].reshape(depth, width))
        for i in range(nx)
    ]


def ring_panel(places, panels):
    order = (0, 1, 3, 2, 4)
    return [
        (pl.multiple_of(places[i], panel.shape[0]), panel[...]) for i, panel in zip(order, panels)
    ]


def product_kernel(pieces, places, rows_ref, sum_ref, *refs):
    comps, dates = rows_ref.shape
    panels, out_ref = refs[:-1], refs[-1]
    parts = pieces(places, panels)
    state_sum = sum(jnp.sum(part.astype(jnp.float32), axis=0, keepdims=True) for _, part in parts)
    state_mean = state_sum / dates
    for start in range(0, comps, BLOCK):
        block = pl.ds(start, BLOCK)
        acc = sum(
            jnp.dot(
                rows_ref[block, pl.ds(place, part.shape[0])],
                part,
                preferred_element_type=jnp.float32,
            )
            for place, part in parts
        )
        inc_mean = sum_ref[block, :] / dates
        out_ref[block, :] = (acc - dates * (inc_mean * state_mean)) * (1.0 / (dates - 1))


def product(pieces, places, rows, inc_sum, panels, offset, columns, out):
    comps, dates = rows.shape
    width = panels[0].shape[-1]
    tile = TILE if width % TILE == 0 and offset % TILE == 0 else TILE // 2
    base = offset // tile
    whole = pl.Buffered(1)
    in_specs = [
        pl.BlockSpec(memory_space=pltpu.SMEM),
        pl.BlockSpec(rows.shape, lambda j: (0, 0), pipeline_mode=whole),
        pl.BlockSpec(inc_sum.shape, lambda j: (0, 0), pipeline_mode=whole),
    ]
    for panel in panels:
        lead = (0,) * (panel.ndim - 1)
        in_specs.append(pl.BlockSpec(panel.shape[:-1] + (tile,), lambda j, lead=lead: lead + (j,)))
    args = [places, rows, inc_sum] + panels
    aliases = {}
    kernel = functools.partial(product_kernel, pieces)
    if out is not None:
        in_specs.append(pl.BlockSpec(memory_space=pl.ANY))
        aliases = {len(args): 0}
        args.append(out)

        def kernel(*refs):
            product_kernel(pieces, *refs[:-2], refs[-1])

    return pl.pallas_call(
        kernel,
        out_shape=jax.ShapeDtypeStruct((comps, columns), jnp.float32),
        grid=(width // tile,),
        in_specs=in_specs,
        out_specs=pl.BlockSpec((comps, tile), lambda j: (0, base + j)),
        input_output_aliases=aliases,
        compiler_params=pltpu.CompilerParams(vmem_limit_bytes=60 * 2**20),
        cost_estimate=pl.CostEstimate(
            flops=2 * comps * dates * width * WEIGHT,
            bytes_accessed=(2 * comps * dates + 2 * dates * width + 4 * comps * width) * WEIGHT,
            transcendentals=0,
        ),
        name="product",
    )(*args)


def group_places(group_date, group):
    per = group_date.shape[0] // NCOL
    col = lax.axis_index("col")
    y, zl, c = col // (2 * NC), (col // NC) % 2, col % NC
    owner = group_date // per
    oy, oz, oc = owner // (2 * NC), (owner // NC) % 2, owner % NC
    place = ((((oc + c) % 2) * NY + (oy - y + NY) % NY) * 2 + (oz + zl) % 2) * per + group_date % per
    return (place * group).astype(jnp.int32)


def body(increments, states, group_date):
    group, total = states.shape
    columns = total // NCOL
    dates = group * group_date.shape[0]
    barrier = lax.optimization_barrier

    def exchange(sent):
        return lax.all_to_all(sent, AXES, 0, 0, tiled=True, axis_index_groups=SAME_X)

    wa, wb, wc = WIDTHS
    x = lax.axis_index("row") // 2
    depth = dates // NX
    places = jnp.stack(
        [(x + step) % NX * depth for step in range(NX)] + [(x + 2) % NX * depth + depth // 2]
    ).astype(jnp.int32)

    cut = depth // 2
    starts = group_places(group_date, group)

    raw = pick(states, 0, wa, 1)
    raw_left = lax.ppermute(raw, AXES, X_UP)
    raw_right = lax.ppermute(raw, AXES, X_DOWN)
    raw_far = lax.ppermute(raw, AXES, X_FAR)
    pair = lax.ppermute(increments, AXES, Z_PAIR)
    sentb = pick(states, wa, wb, 2)
    gotc = exchange(pick(states, wa + wb, wc, 2)).reshape(-1, wc)

    sentb, raw, raw_left, raw_right, raw_far, gotc, increments, pair = barrier(
        (sentb, raw, raw_left, raw_right, raw_far, gotc, increments, pair)
    )
    left = lax.ppermute(gotc, AXES, X_UP)
    right = lax.ppermute(gotc, AXES, X_DOWN)
    near = jnp.stack([increments, pair])
    below = lax.ppermute(near, AXES, Y_UP)
    above = lax.ppermute(near, AXES, Y_DOWN)
    across = lax.ppermute(near, AXES, Y_FAR)
    gotb = exchange(sentb).reshape(-1, wb)
    senta = join([raw, raw_right, raw_far, raw_left])

    senta, gotb, gotc, left, right, to_right, to_left = barrier(
        (senta, gotb, gotc, left, right, left[:cut], right[cut:])
    )
    far_left = lax.ppermute(to_right, AXES, X_UP)
    far_right = lax.ppermute(to_left, AXES, X_DOWN)
    left_b = lax.ppermute(gotb, AXES, X_UP)
    right_b = lax.ppermute(gotb, AXES, X_DOWN)
    mine = jnp.stack([near, above, across, below]).reshape(dates // 2, -1)
    other = lax.ppermute(mine, AXES, CORE)
    gota = exchange(senta).reshape(2 * NCOL, NX, group, wa)
    rows, inc_sum = align(starts, mine, other)
    ring = [gotc, right, left, far_left, far_right]
    out = product(ring_panel, places, rows, inc_sum, ring, wa + wb, columns, None)

    left_b, right_b, out = barrier((left_b, right_b, out))
    far_left_b = lax.ppermute(left_b[:cut], AXES, X_UP)
    far_right_b = lax.ppermute(right_b[cut:], AXES, X_DOWN)
    out = product(exchange_panel, places, rows, inc_sum, [gota], 0, columns, out)
    ring = [gotb, right_b, left_b, far_left_b, far_right_b]
    return product(ring_panel, places, rows, inc_sum, ring, wa, columns, out)


def solution(mesh):
    in_specs = (P("col", "row"), P(("row", "col"), None), P())
    out_specs = P("row", "col")
    return jax.shard_map(body, mesh=mesh, in_specs=in_specs, out_specs=out_specs, check_vma=False)
```

time: 192 us -> 182 us (0.948)
  blocking collectives: 28.8 us -> 0 us
  starting transfers between devices: 27.1 us -> 45.7 us
  between operations: 13.5 us -> 0.17 us
  Pallas kernels: 39.1 us -> 50.5 us
  waiting for transfers between devices: 64.4 us -> 74.3 us
  local copies, waits for them, and re-layouts: 14.5 us -> 7.98 us
    all_to_all x1 -> x0, blocking collectives: 28.8 us -> none  [exchange(): lax.all_to_all(both, AXES, 0, 0, tiled=True, axis_index_groups=SAME_X)]
    ppermute x2 -> x11, waiting for transfers between devices: 27.3 us -> 49.8 us  [the longest x1 20.4 us: body(): right_b = lax.ppermute(gotb, AXES, X_DOWN)]
    pallas_call x0 -> x4, Pallas kernels: none -> 11 us  [the longest x3 6.83 us: pick(): pl.pallas_call(functools.partial(pick_kernel, offset), out_shape=jax.Shap...]
    ppermute x2 -> x11, starting transfers between devices: 3.49 us -> 14.5 us  [the longest x1 2.15 us: body(): across = lax.ppermute(near, AXES, Y_FAR)]
    ppermute x1, waiting for transfers between devices: 10.1 us -> 0.01 us  [body(): raw_left = lax.ppermute(raw, AXES, X_UP)]
    all_to_all x2 -> x3, starting transfers between devices: 15.2 us -> 23.4 us  [exchange(): lax.all_to_all(sent, AXES, 0, 0, tiled=True, axis_index_groups=SAME_X)]
    ppermute x1, waiting for transfers between devices: 10.5 us -> 4.23 us  [body(): raw_right = lax.ppermute(raw, AXES, X_DOWN)]
    ppermute x1, waiting for transfers between devices: 0.01 us -> 5.71 us  [body(): right = lax.ppermute(gotc, AXES, X_DOWN)]
  transfers between devices with their start and end apart: 11 -> 19, of which waited for: 8 -> 13; matrix products, arithmetic and copies ran while one was open for 8% -> 5% of each run, Pallas kernels for 14% -> 20%
where the time goes in v2:
time: 182 us; the launch traced here: 181 us
  waiting for transfers between devices  74.3 us (41%)
  Pallas kernels  50.5 us (28%)
  starting transfers between devices  45.7 us (25%)
  local copies, waits for them, and re-layouts  7.98 us (4%)
  other arithmetic  2.29 us (1%)
    pallas_call x3, Pallas kernels, product(): pl.pallas_call(kernel, out_shape=jax.ShapeDtypeStruct((comps, columns), j...  33.1 us
    all_to_all x3, starting transfers between devices, exchange(): lax.all_to_all(sent, AXES, 0, 0, tiled=True, axis_index_groups=SAME_X)  23.4 us
    ppermute x1, waiting for transfers between devices, body(): right_b = lax.ppermute(gotb, AXES, X_DOWN)  20.4 us
    ppermute x1, waiting for transfers between devices, body(): pair = lax.ppermute(increments, AXES, Z_PAIR)  14 us
    all_to_all x3, waiting for transfers between devices, exchange(): lax.all_to_all(sent, AXES, 0, 0, tiled=True, axis_index_groups=SAME_X)  12.3 us
    ppermute x1, waiting for transfers between devices, body(): above = lax.ppermute(near, AXES, Y_DOWN)  10.2 us
    pallas_call x3, Pallas kernels, pick(): pl.pallas_call(functools.partial(pick_kernel, offset), out_shape=jax.Shap...  6.83 us
    pallas_call x1, Pallas kernels, align(): pl.pallas_call(align_kernel, out_shape=(jax.ShapeDtypeStruct((comps, date...  6.34 us
  transfers between devices with their start and end apart: 19, of which 13 were waited for; matrix products, arithmetic and copies ran while one was open for 5% of the time, Pallas kernels for 20%

profile of v2, /device:TPU:8, one launch (start us, length us, event | category | flops | bytes accessed | tf_op | source)
XLA Modules:
  0.0 180.8 jit_solution(14453834557157278056)
XLA Ops:
  0.0 2.4 %pick.5 = bf16[32,16,1536]{2,1,0:T(8,128)(2,1)} custom-call(bf16[16,65536]{1,0:T(8,128)(2,1)} %states_ref.5), custom_call_target="tpu_custom_call" | custom-call | flops 1536 | bytes 1536 | tf_op jit(solution)/shard_map/pick/pallas_call | solution.py:70
  2.4 8.6 %all-to-all-start = ((bf16[32,16,1536]{2,1,0:T(8,128)(2,1)}), bf16[32,16,1536]{2,1,0:T(8,128)(2,1)}, u32[]{:S(2)}, u32[]{:S(2)}) async-start(bf16[32,16,1536]{2,1,0:T(8,128)(2,1)} %pick.5), calls=%async_computation | async-start | bytes 3145728 | tf_op jit(solution)/shard_map/all_to_all | solution.py:257
  11.0 2.0 %pick.4.refs_0_ = bf16[16,16,1024]{2,1,0:T(8,128)(2,1)} custom-call(bf16[16,65536]{1,0:T(8,128)(2,1)} %states_ref.5), custom_call_target="tpu_custom_call" | custom-call | flops 1024 | bytes 1024 | tf_op jit(solution)/shard_map/pick/pallas_call | solution.py:70
  13.0 3.1 %collective-permute-start.2 = (bf16[16,16,1024]{2,1,0:T(8,128)(2,1)}, bf16[16,16,1024]{2,1,0:T(8,128)(2,1)S(1)}, u32[]{:S(2)}, u32[]{:S(2)}) collective-permute-start(bf16[16,16,1024]{2,1,0:T(8,128)(2,1)} %pick.4.refs_0_), channel_id=1, source_target_pairs={{0,64},{1,65},{2,66},{3,67},{16,80},{17,81},{18,82},{19,83},{4,68}... | collective-permute-start | bytes 1572872 | tf_op jit(solution)/shard_map/ppermute | solution.py:272
  16.1 1.1 collective-permute-start.1
  17.3 0.9 collective-permute-start
  18.2 1.5 collective-permute-start.3
  19.6 2.4 %pick.3 = bf16[32,16,1536]{2,1,0:T(8,128)(2,1)} custom-call(bf16[16,65536]{1,0:T(8,128)(2,1)} %states_ref.5), custom_call_target="tpu_custom_call" | custom-call | flops 1536 | bytes 1536 | tf_op jit(solution)/shard_map/pick/pallas_call | solution.py:70
  22.1 14.0 %collective-permute-done.3 = bf16[128,1024]{1,0:T(8,128)(2,1)S(1)} collective-permute-done((bf16[128,1024]{1,0:T(8,128)(2,1)S(1)}, bf16[128,1024]{1,0:T(8,128)(2,1)S(1)}, u32[]{:S(2)}, u32[]{:S(2)}) %collective-permute-start.3) | collective-permute-done | bytes 262176 | tf_op jit(solution)/shard_map/ppermute | solution.py:273
  36.1 4.2 %collective-permute-done.1.refs_1_ = bf16[16,16,1024]{2,1,0:T(8,128)(2,1)} collective-permute-done((bf16[16,16,1024]{2,1,0:T(8,128)(2,1)}, bf16[16,16,1024]{2,1,0:T(8,128)(2,1)}, u32[]{:S(2)}, u32[]{:S(2)}) %collective-permute-start.1) | collective-permute-done | bytes 524320 | tf_op jit(solution)/shard_map/ppermute | solution.py:271
  40.4 2.2 %collective-permute-start.5 = (bf16[2,128,1024]{2,1,0:T(8,128)(2,1)S(1)}, bf16[2,128,1024]{2,1,0:T(8,128)(2,1)S(1)}, u32[]{:S(2)}, u32[]{:S(2)}) collective-permute-start(bf16[2,128,1024]{2,1,0:T(8,128)(2,1)S(1)} %get-tuple-element.46), channel_id=1, source_target_pairs={{0,8},{1,9},{2,10},{3,11},{16,24},{17,25},{18,26},{19,27},{4,12},{... | collective-permute-start | bytes 1572872 | tf_op jit(solution)/shard_map/ppermute | solution.py:285
  42.5 1.5 collective-permute-start.4
  44.0 0.6 collective-permute-start.6
  44.5 2.6 %collective-permute-start.9 = (bf16[512,1536]{1,0:T(8,128)(2,1)}, bf16[512,1536]{1,0:T(8,128)(2,1)}, u32[]{:S(2)}, u32[]{:S(2)}) collective-permute-start(bf16[512,1536]{1,0:T(8,128)(2,1)} %bitcast.5.refs_0_), channel_id=1, source_target_pairs={{0,96},{1,97},{2,98},{3,99},{16,112},{17,113},{18,114},{19,115},{4... | collective-permute-start | bytes 4718600 | tf_op jit(solution)/shard_map/ppermute | solution.py:281
  47.2 7.7 %all-to-all-start.1 = ((bf16[32,16,1536]{2,1,0:T(8,128)(2,1)}), bf16[32,16,1536]{2,1,0:T(8,128)(2,1)}, u32[]{:S(2)}, u32[]{:S(2)}) async-start(bf16[32,16,1536]{2,1,0:T(8,128)(2,1)} %pick.3), calls=%async_computation.1 | async-start | bytes 3145728 | tf_op jit(solution)/shard_map/all_to_all | solution.py:257
  54.9 1.9 %collective-permute-done.5 = bf16[2,128,1024]{2,1,0:T(8,128)(2,1)S(1)} collective-permute-done((bf16[2,128,1024]{2,1,0:T(8,128)(2,1)S(1)}, bf16[2,128,1024]{2,1,0:T(8,128)(2,1)S(1)}, u32[]{:S(2)}, u32[]{:S(2)}) %collective-permute-start.5) | collective-permute-done | bytes 524320 | tf_op jit(solution)/shard_map/ppermute | solution.py:285
  56.8 10.2 %collective-permute-done.4 = bf16[2,128,1024]{2,1,0:T(8,128)(2,1)S(1)} collective-permute-done((bf16[2,128,1024]{2,1,0:T(8,128)(2,1)S(1)}, bf16[2,128,1024]{2,1,0:T(8,128)(2,1)S(1)}, u32[]{:S(2)}, u32[]{:S(2)}) %collective-permute-start.4) | collective-permute-done | bytes 524320 | tf_op jit(solution)/shard_map/ppermute | solution.py:284
  67.0 1.0 collective-permute-done.6
  68.0 0.8 copy-done.4
  68.8 1.6 pad_maximum_fusion
  70.5 0.1 collective-permute-start.7
  70.6 4.2 %join.1 = bf16[32,4,16,1024]{3,2,1,0:T(8,128)(2,1)} custom-call(bf16[16,16,1024]{2,1,0:T(8,128)(2,1)} %pick.4.refs_0_, bf16[16,16,1024]{2,1,0:T(8,128)(2,1)} %collective-permute-done.1.refs_1_, bf16[16,16,1024]{2,1,0:T(8,128)(2,1)} %copy-done.1, bf16[16,16,1024]{2,1,0:T(8,128)(2,1)} %collective-permute-done.refs_3_), custom_call_target="tpu_custom_call" | custom-call | flops 1024 | bytes 1024 | tf_op jit(solution)/shard_map/join/pallas_call | solution.py:91
  74.8 5.7 %collective-permute-done.9.refs_1_ = bf16[512,1536]{1,0:T(8,128)(2,1)} collective-permute-done((bf16[512,1536]{1,0:T(8,128)(2,1)}, bf16[512,1536]{1,0:T(8,128)(2,1)}, u32[]{:S(2)}, u32[]{:S(2)}) %collective-permute-start.9) | collective-permute-done | bytes 1572896 | tf_op jit(solution)/shard_map/ppermute | solution.py:281
  80.5 1.2 slice.17
  81.7 2.2 %collective-permute-done.8.refs_2_ = bf16[512,1536]{1,0:T(8,128)(2,1)} collective-permute-done((bf16[512,1536]{1,0:T(8,128)(2,1)}, bf16[512,1536]{1,0:T(8,128)(2,1)}, u32[]{:S(2)}, u32[]{:S(2)}) %collective-permute-start.8) | collective-permute-done | bytes 1572896 | tf_op jit(solution)/shard_map/ppermute | solution.py:280
  83.9 2.1 %slice.16 = bf16[256,1536]{1,0:T(8,128)(2,1)} slice(bf16[512,1536]{1,0:T(8,128)(2,1)} %collective-permute-done.8.refs_2_), slice={[0:256], [0:1536]} | slice | bytes 1572864 | tf_op jit(solution)/shard_map/slice | solution.py:290
  86.0 0.7 all-to-all-done.1
  86.6 1.5 collective-permute-start.12
  88.1 1.7 collective-permute-start.13
  89.9 0.7 stack.47.places.refs_0_
  90.5 0.6 fusion.10.starts
  91.1 1.7 collective-permute-start.11
  92.9 0.3 collective-permute-start.10
  93.2 7.1 %all-to-all-start.2 = ((bf16[32,4,16,1024]{3,2,1,0:T(8,128)(2,1)}), bf16[32,4,16,1024]{3,2,1,0:T(8,128)(2,1)}, u32[]{:S(2)}, u32[]{:S(2)}) async-start(bf16[32,4,16,1024]{3,2,1,0:T(8,128)(2,1)} %join.1), calls=%async_computation.2 | async-start | bytes 8388608 | tf_op jit(solution)/shard_map/all_to_all | solution.py:257
  100.3 6.3 %align.1 = (bf16[1024,2048]{1,0:T(8,128)(2,1)}, f32[1024,1]{1,0:T(8,128)}) custom-call(s32[128]{0:T(128)} %fusion.10.starts, bf16[1024,1024]{1,0:T(8,128)(2,1)} %bitcast.16, bf16[1024,1024]{1,0:T(8,128)(2,1)} %collective-permute-done.7.other_ref), custom_call_target="tpu_custom_call" | custom-call | flops 1024 | bytes 1024 | tf_op jit(solution)/shard_map/align/pallas_call | solution.py:140
  106.6 2.0 %collective-permute-done.12.refs_3_ = bf16[256,1536]{1,0:T(8,128)(2,1)} collective-permute-done((bf16[256,1536]{1,0:T(8,128)(2,1)}, bf16[256,1536]{1,0:T(8,128)(2,1)}, u32[]{:S(2)}, u32[]{:S(2)}) %collective-permute-start.12) | collective-permute-done | bytes 786464 | tf_op jit(solution)/shard_map/ppermute | solution.py:292
  108.6 0.1 collective-permute-done.13.refs_4_
  108.7 12.0 %product.3.refs_4_ = f32[1024,4096]{1,0:T(8,128)} custom-call(s32[5]{0:T(128)} %stack.47.places.refs_0_, bf16[1024,2048]{1,0:T(8,128)(2,1)} %get-tuple-element.27.rows_ref.refs_1_, f32[1024,1]{1,0:T(8,128)} %get-tuple-element.28.sum_ref.refs_2_, bf16[512,1536]{1,0:T(8,128)(2,1)} %bitcast.5.refs_0_, bf16[512,1536]{1,0:T(8,128)(2,1)} %collective-permute-done.9.refs_1_, ...), custom_call_target="tpu_custom_call" | custom-call | flops 51539607552 | bytes 134217728 | tf_op jit(solution)/shard_map/product/pallas_call | solution.py:223
  120.7 20.4 %collective-permute-done.11.refs_4_ = bf16[512,1536]{1,0:T(8,128)(2,1)} collective-permute-done((bf16[512,1536]{1,0:T(8,128)(2,1)}, bf16[512,1536]{1,0:T(8,128)(2,1)}, u32[]{:S(2)}, u32[]{:S(2)}) %collective-permute-start.11) | collective-permute-done | bytes 1572896 | tf_op jit(solution)/shard_map/ppermute | solution.py:295
  141.1 0.2 collective-permute-done.10.refs_5_
  141.3 1.2 slice.15
  142.5 1.2 slice.14
  143.7 1.5 collective-permute-start.14
  145.3 2.0 %collective-permute-start.15 = (bf16[256,1536]{1,0:T(8,128)(2,1)S(1)}, bf16[256,1536]{1,0:T(8,128)(2,1)}, u32[]{:S(2)}, u32[]{:S(2)}) collective-permute-start(bf16[256,1536]{1,0:T(8,128)(2,1)S(1)} %slice.15), channel_id=1, source_target_pairs={{0,96},{1,97},{2,98},{3,99},{16,112},{17,113},{18,114},{19,115},{4... | collective-permute-start | bytes 2359304 | tf_op jit(solution)/shard_map/ppermute | solution.py:305
  147.2 11.6 %all-to-all-done.2.refs_3_ = bf16[32,4,16,1024]{3,2,1,0:T(8,128)(2,1)} async-done(((bf16[32,4,16,1024]{3,2,1,0:T(8,128)(2,1)}), bf16[32,4,16,1024]{3,2,1,0:T(8,128)(2,1)}, u32[]{:S(2)}, u32[]{:S(2)}) %all-to-all-start.2) | async-done | bytes 4194336 | tf_op jit(solution)/shard_map/all_to_all | solution.py:257
  158.8 9.1 %product.4.refs_8_ = f32[1024,4096]{1,0:T(8,128)} custom-call(s32[5]{0:T(128)} %stack.47.places.refs_0_, bf16[1024,2048]{1,0:T(8,128)(2,1)} %get-tuple-element.27.rows_ref.refs_1_, f32[1024,1]{1,0:T(8,128)} %get-tuple-element.28.sum_ref.refs_2_, bf16[32,4,16,1024]{3,2,1,0:T(8,128)(2,1)} %all-to-all-done.2.refs_3_, ...), custom_call_target="tpu_custom_call", output_to_operand_aliasing={{}: (4, {})} | custom-call | flops 34359738368 | bytes 100663296 | tf_op jit(solution)/shard_map/product/pallas_call | solution.py:223
  167.9 0.9 copy-done.7
  168.8 12.0 %product.5 = f32[1024,4096]{1,0:T(8,128)} custom-call(s32[5]{0:T(128)} %stack.47.places.refs_0_, bf16[1024,2048]{1,0:T(8,128)(2,1)} %get-tuple-element.27.rows_ref.refs_1_, f32[1024,1]{1,0:T(8,128)} %get-tuple-element.28.sum_ref.refs_2_, bf16[512,1536]{1,0:T(8,128)(2,1)} %bitcast.13.refs_3_, ...), custom_call_target="tpu_custom_call", output_to_operand_aliasing={{}: (8, {})} | custom-call | flops 51539607552 | bytes 134217728 | tf_op jit(solution)/shard_map/product/pallas_call | solution.py:223
  (22 shorter events, 0.1 us)
Async XLA Ops:
  2.4 37.9 %all-to-all-start = ((bf16[32,16,1536]{2,1,0:T(8,128)(2,1)}), bf16[32,16,1536]{2,1,0:T(8,128)(2,1)}, u32[]{:S(2)}, u32[]{:S(2)}) async-start(bf16[32,16,1536]{2,1,0:T(8,128)(2,1)} %pick.5), calls=%async_computation | async-start | bytes 3145728 | tf_op jit(solution)/shard_map/all_to_all | solution.py:257
  11.0 7.1 %copy-start.5 = (bf16[128,1024]{1,0:T(8,128)(2,1)S(1)}, bf16[128,1024]{1,0:T(8,128)(2,1)}, u32[]{:S(2)}) copy-start(bf16[128,1024]{1,0:T(8,128)(2,1)} %param.3) | copy-start | bytes 786436
  13.0 23.0 %collective-permute-start.2 = (bf16[16,16,1024]{2,1,0:T(8,128)(2,1)}, bf16[16,16,1024]{2,1,0:T(8,128)(2,1)S(1)}, u32[]{:S(2)}, u32[]{:S(2)}) collective-permute-start(bf16[16,16,1024]{2,1,0:T(8,128)(2,1)} %pick.4.refs_0_), channel_id=1, source_target_pairs={{0,64},{1,65},{2,66},{3,67},{16,80},{17,81},{18,82},{19,83},{4,68}... | collective-permute-start | bytes 1572872 | tf_op jit(solution)/shard_map/ppermute | solution.py:272
  16.1 24.1 %collective-permute-start.1 = (bf16[16,16,1024]{2,1,0:T(8,128)(2,1)}, bf16[16,16,1024]{2,1,0:T(8,128)(2,1)}, u32[]{:S(2)}, u32[]{:S(2)}) collective-permute-start(bf16[16,16,1024]{2,1,0:T(8,128)(2,1)} %pick.4.refs_0_), channel_id=1, source_target_pairs={{0,96},{1,97},{2,98},{3,99},{16,112},{17,113},{18,114},{19,115},{4... | collective-permute-start | bytes 1572872 | tf_op jit(solution)/shard_map/ppermute | solution.py:271
  17.3 23.0 %collective-permute-start = (bf16[16,16,1024]{2,1,0:T(8,128)(2,1)}, bf16[16,16,1024]{2,1,0:T(8,128)(2,1)}, u32[]{:S(2)}, u32[]{:S(2)}) collective-permute-start(bf16[16,16,1024]{2,1,0:T(8,128)(2,1)} %pick.4.refs_0_), channel_id=1, source_target_pairs={{0,32},{1,33},{2,34},{3,35},{16,48},{17,49},{18,50},{19,51},{4,36}... | collective-permute-start | bytes 1572872 | tf_op jit(solution)/shard_map/ppermute | solution.py:270
  18.2 17.9 %collective-permute-start.3 = (bf16[128,1024]{1,0:T(8,128)(2,1)S(1)}, bf16[128,1024]{1,0:T(8,128)(2,1)S(1)}, u32[]{:S(2)}, u32[]{:S(2)}) collective-permute-start(bf16[128,1024]{1,0:T(8,128)(2,1)S(1)} %copy-done.5), channel_id=1, source_target_pairs={{0,2},{1,3},{2,0},{3,1},{16,18},{17,19},{18,16},{19,17},{4,6},{5,7... | collective-permute-start | bytes 786440 | tf_op jit(solution)/shard_map/ppermute | solution.py:273
  36.0 11.1 %copy-start.1 = (bf16[16,16,1024]{2,1,0:T(8,128)(2,1)}, bf16[16,16,1024]{2,1,0:T(8,128)(2,1)S(1)}, u32[]{:S(2)}) copy-start(bf16[16,16,1024]{2,1,0:T(8,128)(2,1)S(1)} %collective-permute-done.2.refs_2_) | copy-start | bytes 1572868
  40.4 16.4 %collective-permute-start.5 = (bf16[2,128,1024]{2,1,0:T(8,128)(2,1)S(1)}, bf16[2,128,1024]{2,1,0:T(8,128)(2,1)S(1)}, u32[]{:S(2)}, u32[]{:S(2)}) collective-permute-start(bf16[2,128,1024]{2,1,0:T(8,128)(2,1)S(1)} %get-tuple-element.46), channel_id=1, source_target_pairs={{0,8},{1,9},{2,10},{3,11},{16,24},{17,25},{18,26},{19,27},{4,12},{... | collective-permute-start | bytes 1572872 | tf_op jit(solution)/shard_map/ppermute | solution.py:285
  42.5 24.5 %collective-permute-start.4 = (bf16[2,128,1024]{2,1,0:T(8,128)(2,1)S(1)}, bf16[2,128,1024]{2,1,0:T(8,128)(2,1)S(1)}, u32[]{:S(2)}, u32[]{:S(2)}) collective-permute-start(bf16[2,128,1024]{2,1,0:T(8,128)(2,1)S(1)} %get-tuple-element.46), channel_id=1, source_target_pairs={{0,12},{1,13},{2,14},{3,15},{16,28},{17,29},{18,30},{19,31},{4,0},... | collective-permute-start | bytes 1572872 | tf_op jit(solution)/shard_map/ppermute | solution.py:284
  44.0 24.1 %collective-permute-start.6 = (bf16[2,128,1024]{2,1,0:T(8,128)(2,1)S(1)}, bf16[2,128,1024]{2,1,0:T(8,128)(2,1)S(1)}, u32[]{:S(2)}, u32[]{:S(2)}) collective-permute-start(bf16[2,128,1024]{2,1,0:T(8,128)(2,1)S(1)} %get-tuple-element.46), channel_id=1, source_target_pairs={{0,4},{1,5},{2,6},{3,7},{16,20},{17,21},{18,22},{19,23},{4,8},{5,9... | collective-permute-start | bytes 1572872 | tf_op jit(solution)/shard_map/ppermute | solution.py:283
  44.5 35.9 %collective-permute-start.9 = (bf16[512,1536]{1,0:T(8,128)(2,1)}, bf16[512,1536]{1,0:T(8,128)(2,1)}, u32[]{:S(2)}, u32[]{:S(2)}) collective-permute-start(bf16[512,1536]{1,0:T(8,128)(2,1)} %bitcast.5.refs_0_), channel_id=1, source_target_pairs={{0,96},{1,97},{2,98},{3,99},{16,112},{17,113},{18,114},{19,115},{4... | collective-permute-start | bytes 4718600 | tf_op jit(solution)/shard_map/ppermute | solution.py:281
  47.2 36.7 %collective-permute-start.8 = (bf16[512,1536]{1,0:T(8,128)(2,1)}, bf16[512,1536]{1,0:T(8,128)(2,1)}, u32[]{:S(2)}, u32[]{:S(2)}) collective-permute-start(bf16[512,1536]{1,0:T(8,128)(2,1)} %bitcast.5.refs_0_), channel_id=1, source_target_pairs={{0,32},{1,33},{2,34},{3,35},{16,48},{17,49},{18,50},{19,51},{4,36}... | collective-permute-start | bytes 4718600 | tf_op jit(solution)/shard_map/ppermute | solution.py:280
  47.2 39.5 %all-to-all-start.1 = ((bf16[32,16,1536]{2,1,0:T(8,128)(2,1)}), bf16[32,16,1536]{2,1,0:T(8,128)(2,1)}, u32[]{:S(2)}, u32[]{:S(2)}) async-start(bf16[32,16,1536]{2,1,0:T(8,128)(2,1)} %pick.3), calls=%async_computation.1 | async-start | bytes 3145728 | tf_op jit(solution)/shard_map/all_to_all | solution.py:257
  56.8 11.2 %copy-start.2 = (bf16[2,128,1024]{2,1,0:T(8,128)(2,1)}, bf16[2,128,1024]{2,1,0:T(8,128)(2,1)S(1)}, u32[]{:S(2)}) copy-start(bf16[2,128,1024]{2,1,0:T(8,128)(2,1)S(1)} %collective-permute-done.5) | copy-start | bytes 1572868
  67.0 1.1 copy-start.3
  68.0 0.8 copy-start.4
  70.4 4.3 %copy-start = (bf16[4,2,128,1024]{3,2,1,0:T(8,128)(2,1)}, bf16[4,2,128,1024]{3,2,1,0:T(8,128)(2,1)S(1)}, u32[]{:S(2)}) copy-start(bf16[4,2,128,1024]{3,2,1,0:T(8,128)(2,1)S(1)} %pad_maximum_fusion) | copy-start | bytes 6291460
  70.5 29.8 %collective-permute-start.7 = (bf16[1024,1024]{1,0:T(8,128)(2,1)S(1)}, bf16[1024,1024]{1,0:T(8,128)(2,1)}, u32[]{:S(2)}, u32[]{:S(2)}) collective-permute-start(bf16[1024,1024]{1,0:T(8,128)(2,1)S(1)} %bitcast.15), channel_id=1, source_target_pairs={{0,1},{1,0},{2,3},{3,2},{16,17},{17,16},{18,19},{19,18},{4,5},{5,4... | collective-permute-start | bytes 6291464 | tf_op jit(solution)/shard_map/ppermute | solution.py:297
  74.8 15.8 %copy-start.6 = (s32[128]{0:T(128)S(1)}, s32[128]{0:T(128)}, u32[]{:S(2)}) copy-start(s32[128]{0:T(128)} %param.5) | copy-start | bytes 1540
  86.6 21.9 %collective-permute-start.12 = (bf16[256,1536]{1,0:T(8,128)(2,1)}, bf16[256,1536]{1,0:T(8,128)(2,1)}, u32[]{:S(2)}, u32[]{:S(2)}) collective-permute-start(bf16[256,1536]{1,0:T(8,128)(2,1)} %slice.16), channel_id=1, source_target_pairs={{0,32},{1,33},{2,34},{3,35},{16,48},{17,49},{18,50},{19,51},{4,36}... | collective-permute-start | bytes 2359304 | tf_op jit(solution)/shard_map/ppermute | solution.py:292
  88.1 20.5 %collective-permute-start.13 = (bf16[256,1536]{1,0:T(8,128)(2,1)S(1)}, bf16[256,1536]{1,0:T(8,128)(2,1)}, u32[]{:S(2)}, u32[]{:S(2)}) collective-permute-start(bf16[256,1536]{1,0:T(8,128)(2,1)S(1)} %slice.17), channel_id=1, source_target_pairs={{0,96},{1,97},{2,98},{3,99},{16,112},{17,113},{18,114},{19,115},{4... | collective-permute-start | bytes 2359304 | tf_op jit(solution)/shard_map/ppermute | solution.py:293
  91.1 50.0 %collective-permute-start.11 = (bf16[512,1536]{1,0:T(8,128)(2,1)}, bf16[512,1536]{1,0:T(8,128)(2,1)}, u32[]{:S(2)}, u32[]{:S(2)}) collective-permute-start(bf16[512,1536]{1,0:T(8,128)(2,1)} %bitcast.13.refs_3_), channel_id=1, source_target_pairs={{0,96},{1,97},{2,98},{3,99},{16,112},{17,113},{18,114},{19,115},{4... | collective-permute-start | bytes 4718600 | tf_op jit(solution)/shard_map/ppermute | solution.py:295
  92.9 48.5 %collective-permute-start.10 = (bf16[512,1536]{1,0:T(8,128)(2,1)}, bf16[512,1536]{1,0:T(8,128)(2,1)}, u32[]{:S(2)}, u32[]{:S(2)}) collective-permute-start(bf16[512,1536]{1,0:T(8,128)(2,1)} %bitcast.13.refs_3_), channel_id=1, source_target_pairs={{0,32},{1,33},{2,34},{3,35},{16,48},{17,49},{18,50},{19,51},{4,36}... | collective-permute-start | bytes 4718600 | tf_op jit(solution)/shard_map/ppermute | solution.py:294
  93.2 65.6 %all-to-all-start.2 = ((bf16[32,4,16,1024]{3,2,1,0:T(8,128)(2,1)}), bf16[32,4,16,1024]{3,2,1,0:T(8,128)(2,1)}, u32[]{:S(2)}, u32[]{:S(2)}) async-start(bf16[32,4,16,1024]{3,2,1,0:T(8,128)(2,1)} %join.1), calls=%async_computation.2 | async-start | bytes 8388608 | tf_op jit(solution)/shard_map/all_to_all | solution.py:257
  143.7 24.2 %collective-permute-start.14 = (bf16[256,1536]{1,0:T(8,128)(2,1)S(1)}, bf16[256,1536]{1,0:T(8,128)(2,1)S(1)}, u32[]{:S(2)}, u32[]{:S(2)}) collective-permute-start(bf16[256,1536]{1,0:T(8,128)(2,1)S(1)} %slice.14), channel_id=1, source_target_pairs={{0,32},{1,33},{2,34},{3,35},{16,48},{17,49},{18,50},{19,51},{4,36}... | collective-permute-start | bytes 2359304 | tf_op jit(solution)/shard_map/ppermute | solution.py:304
  145.3 22.7 %collective-permute-start.15 = (bf16[256,1536]{1,0:T(8,128)(2,1)S(1)}, bf16[256,1536]{1,0:T(8,128)(2,1)}, u32[]{:S(2)}, u32[]{:S(2)}) collective-permute-start(bf16[256,1536]{1,0:T(8,128)(2,1)S(1)} %slice.15), channel_id=1, source_target_pairs={{0,96},{1,97},{2,98},{3,99},{16,112},{17,113},{18,114},{19,115},{4... | collective-permute-start | bytes 2359304 | tf_op jit(solution)/shard_map/ppermute | solution.py:305
  167.9 0.9 copy-start.7

commit v3 on v2

--- a/solution.py
+++ b/solution.py
@@ -12,7 +12,7 @@
 NCOL = NY * 2 * NC
 TILE = 512
 BLOCK = 256
-WEIGHT = 8
+WEIGHT = 6
 WIDTHS = (1024, 1536, 1536)
 
 

time: 182 us -> 178 us (0.978)
  waiting for transfers between devices: 74.3 us -> 70.9 us
    all_to_all x3, waiting for transfers between devices: 12.3 us -> 8.99 us  [exchange(): lax.all_to_all(sent, AXES, 0, 0, tiled=True, axis_index_groups=SAME_X)]
where the time goes in v3:
time: 178 us
  waiting for transfers between devices  70.9 us (40%)
  Pallas kernels  50.5 us (28%)
  starting transfers between devices  45.7 us (26%)
  local copies, waits for them, and re-layouts  7.98 us (4%)
  other arithmetic  2.29 us (1%)
    pallas_call x3, Pallas kernels, product(): pl.pallas_call(kernel, out_shape=jax.ShapeDtypeStruct((comps, columns), j...  33.1 us
    all_to_all x3, starting transfers between devices, exchange(): lax.all_to_all(sent, AXES, 0, 0, tiled=True, axis_index_groups=SAME_X)  23.4 us
    ppermute x1, waiting for transfers between devices, body(): right_b = lax.ppermute(gotb, AXES, X_DOWN)  20.5 us
    ppermute x1, waiting for transfers between devices, body(): pair = lax.ppermute(increments, AXES, Z_PAIR)  14 us
    ppermute x1, waiting for transfers between devices, body(): above = lax.ppermute(near, AXES, Y_DOWN)  10.2 us
    all_to_all x3, waiting for transfers between devices, exchange(): lax.all_to_all(sent, AXES, 0, 0, tiled=True, axis_index_groups=SAME_X)  8.99 us
    pallas_call x3, Pallas kernels, pick(): pl.pallas_call(functools.partial(pick_kernel, offset), out_shape=jax.Shap...  6.83 us
    pallas_call x1, Pallas kernels, align(): pl.pallas_call(align_kernel, out_shape=(jax.ShapeDtypeStruct((comps, date...  6.36 us
  transfers between devices with their start and end apart: 19, of which 13 were waited for; matrix products, arithmetic and copies ran while one was open for 5% of the time, Pallas kernels for 20%

profile of v3, /device:TPU:8, one launch (start us, length us, event | category | flops | bytes accessed | tf_op | source)
XLA Modules:
  0.0 177.5 jit_solution(10687924294209721697)
XLA Ops:
  0.0 2.4 %pick.5 = bf16[32,16,1536]{2,1,0:T(8,128)(2,1)} custom-call(bf16[16,65536]{1,0:T(8,128)(2,1)} %states_ref.5), custom_call_target="tpu_custom_call" | custom-call | flops 1536 | bytes 1536 | tf_op jit(solution)/shard_map/pick/pallas_call | solution.py:70
  2.4 8.6 %all-to-all-start = ((bf16[32,16,1536]{2,1,0:T(8,128)(2,1)}), bf16[32,16,1536]{2,1,0:T(8,128)(2,1)}, u32[]{:S(2)}, u32[]{:S(2)}) async-start(bf16[32,16,1536]{2,1,0:T(8,128)(2,1)} %pick.5), calls=%async_computation | async-start | bytes 3145728 | tf_op jit(solution)/shard_map/all_to_all | solution.py:257
  11.0 2.0 %pick.4.refs_0_ = bf16[16,16,1024]{2,1,0:T(8,128)(2,1)} custom-call(bf16[16,65536]{1,0:T(8,128)(2,1)} %states_ref.5), custom_call_target="tpu_custom_call" | custom-call | flops 1024 | bytes 1024 | tf_op jit(solution)/shard_map/pick/pallas_call | solution.py:70
  13.0 3.1 %collective-permute-start.2 = (bf16[16,16,1024]{2,1,0:T(8,128)(2,1)}, bf16[16,16,1024]{2,1,0:T(8,128)(2,1)S(1)}, u32[]{:S(2)}, u32[]{:S(2)}) collective-permute-start(bf16[16,16,1024]{2,1,0:T(8,128)(2,1)} %pick.4.refs_0_), channel_id=1, source_target_pairs={{0,64},{1,65},{2,66},{3,67},{16,80},{17,81},{18,82},{19,83},{4,68}... | collective-permute-start | bytes 1572872 | tf_op jit(solution)/shard_map/ppermute | solution.py:272
  16.1 1.1 collective-permute-start.1
  17.3 0.9 collective-permute-start
  18.2 1.5 collective-permute-start.3
  19.6 2.4 %pick.3 = bf16[32,16,1536]{2,1,0:T(8,128)(2,1)} custom-call(bf16[16,65536]{1,0:T(8,128)(2,1)} %states_ref.5), custom_call_target="tpu_custom_call" | custom-call | flops 1536 | bytes 1536 | tf_op jit(solution)/shard_map/pick/pallas_call | solution.py:70
  22.1 14.0 %collective-permute-done.3 = bf16[128,1024]{1,0:T(8,128)(2,1)S(1)} collective-permute-done((bf16[128,1024]{1,0:T(8,128)(2,1)S(1)}, bf16[128,1024]{1,0:T(8,128)(2,1)S(1)}, u32[]{:S(2)}, u32[]{:S(2)}) %collective-permute-start.3) | collective-permute-done | bytes 262176 | tf_op jit(solution)/shard_map/ppermute | solution.py:273
  36.1 4.2 %collective-permute-done.1.refs_1_ = bf16[16,16,1024]{2,1,0:T(8,128)(2,1)} collective-permute-done((bf16[16,16,1024]{2,1,0:T(8,128)(2,1)}, bf16[16,16,1024]{2,1,0:T(8,128)(2,1)}, u32[]{:S(2)}, u32[]{:S(2)}) %collective-permute-start.1) | collective-permute-done | bytes 524320 | tf_op jit(solution)/shard_map/ppermute | solution.py:271
  40.4 2.2 %collective-permute-start.5 = (bf16[2,128,1024]{2,1,0:T(8,128)(2,1)S(1)}, bf16[2,128,1024]{2,1,0:T(8,128)(2,1)S(1)}, u32[]{:S(2)}, u32[]{:S(2)}) collective-permute-start(bf16[2,128,1024]{2,1,0:T(8,128)(2,1)S(1)} %get-tuple-element.46), channel_id=1, source_target_pairs={{0,8},{1,9},{2,10},{3,11},{16,24},{17,25},{18,26},{19,27},{4,12},{... | collective-permute-start | bytes 1572872 | tf_op jit(solution)/shard_map/ppermute | solution.py:285
  42.5 1.5 collective-permute-start.4
  44.0 0.6 collective-permute-start.6
  44.5 2.6 %collective-permute-start.9 = (bf16[512,1536]{1,0:T(8,128)(2,1)}, bf16[512,1536]{1,0:T(8,128)(2,1)}, u32[]{:S(2)}, u32[]{:S(2)}) collective-permute-start(bf16[512,1536]{1,0:T(8,128)(2,1)} %bitcast.5.refs_0_), channel_id=1, source_target_pairs={{0,96},{1,97},{2,98},{3,99},{16,112},{17,113},{18,114},{19,115},{4... | collective-permute-start | bytes 4718600 | tf_op jit(solution)/shard_map/ppermute | solution.py:281
  47.2 7.7 %all-to-all-start.1 = ((bf16[32,16,1536]{2,1,0:T(8,128)(2,1)}), bf16[32,16,1536]{2,1,0:T(8,128)(2,1)}, u32[]{:S(2)}, u32[]{:S(2)}) async-start(bf16[32,16,1536]{2,1,0:T(8,128)(2,1)} %pick.3), calls=%async_computation.1 | async-start | bytes 3145728 | tf_op jit(solution)/shard_map/all_to_all | solution.py:257
  54.9 1.9 %collective-permute-done.5 = bf16[2,128,1024]{2,1,0:T(8,128)(2,1)S(1)} collective-permute-done((bf16[2,128,1024]{2,1,0:T(8,128)(2,1)S(1)}, bf16[2,128,1024]{2,1,0:T(8,128)(2,1)S(1)}, u32[]{:S(2)}, u32[]{:S(2)}) %collective-permute-start.5) | collective-permute-done | bytes 524320 | tf_op jit(solution)/shard_map/ppermute | solution.py:285
  56.8 10.2 %collective-permute-done.4 = bf16[2,128,1024]{2,1,0:T(8,128)(2,1)S(1)} collective-permute-done((bf16[2,128,1024]{2,1,0:T(8,128)(2,1)S(1)}, bf16[2,128,1024]{2,1,0:T(8,128)(2,1)S(1)}, u32[]{:S(2)}, u32[]{:S(2)}) %collective-permute-start.4) | collective-permute-done | bytes 524320 | tf_op jit(solution)/shard_map/ppermute | solution.py:284
  67.0 1.0 collective-permute-done.6
  68.0 0.8 copy-done.4
  68.8 1.6 pad_maximum_fusion
  70.5 0.1 collective-permute-start.7
  70.6 4.2 %join.1 = bf16[32,4,16,1024]{3,2,1,0:T(8,128)(2,1)} custom-call(bf16[16,16,1024]{2,1,0:T(8,128)(2,1)} %pick.4.refs_0_, bf16[16,16,1024]{2,1,0:T(8,128)(2,1)} %collective-permute-done.1.refs_1_, bf16[16,16,1024]{2,1,0:T(8,128)(2,1)} %copy-done.1, bf16[16,16,1024]{2,1,0:T(8,128)(2,1)} %collective-permute-done.refs_3_), custom_call_target="tpu_custom_call" | custom-call | flops 1024 | bytes 1024 | tf_op jit(solution)/shard_map/join/pallas_call | solution.py:91
  74.8 5.7 %collective-permute-done.9.refs_1_ = bf16[512,1536]{1,0:T(8,128)(2,1)} collective-permute-done((bf16[512,1536]{1,0:T(8,128)(2,1)}, bf16[512,1536]{1,0:T(8,128)(2,1)}, u32[]{:S(2)}, u32[]{:S(2)}) %collective-permute-start.9) | collective-permute-done | bytes 1572896 | tf_op jit(solution)/shard_map/ppermute | solution.py:281
  80.5 1.2 slice.17
  81.7 2.2 %collective-permute-done.8.refs_2_ = bf16[512,1536]{1,0:T(8,128)(2,1)} collective-permute-done((bf16[512,1536]{1,0:T(8,128)(2,1)}, bf16[512,1536]{1,0:T(8,128)(2,1)}, u32[]{:S(2)}, u32[]{:S(2)}) %collective-permute-start.8) | collective-permute-done | bytes 1572896 | tf_op jit(solution)/shard_map/ppermute | solution.py:280
  83.9 2.1 %slice.16 = bf16[256,1536]{1,0:T(8,128)(2,1)} slice(bf16[512,1536]{1,0:T(8,128)(2,1)} %collective-permute-done.8.refs_2_), slice={[0:256], [0:1536]} | slice | bytes 1572864 | tf_op jit(solution)/shard_map/slice | solution.py:290
  86.0 0.7 all-to-all-done.1
  86.6 1.5 collective-permute-start.12
  88.1 1.7 collective-permute-start.13
  89.9 7.1 %all-to-all-start.2 = ((bf16[32,4,16,1024]{3,2,1,0:T(8,128)(2,1)}), bf16[32,4,16,1024]{3,2,1,0:T(8,128)(2,1)}, u32[]{:S(2)}, u32[]{:S(2)}) async-start(bf16[32,4,16,1024]{3,2,1,0:T(8,128)(2,1)} %join.1), calls=%async_computation.2 | async-start | bytes 8388608 | tf_op jit(solution)/shard_map/all_to_all | solution.py:257
  97.1 0.7 stack.47.places.refs_0_
  97.7 0.6 fusion.10.starts
  98.3 0.3 collective-permute-start.11
  98.6 1.8 collective-permute-start.10
  100.4 6.4 %align.1 = (bf16[1024,2048]{1,0:T(8,128)(2,1)}, f32[1024,1]{1,0:T(8,128)}) custom-call(s32[128]{0:T(128)} %fusion.10.starts, bf16[1024,1024]{1,0:T(8,128)(2,1)} %bitcast.16, bf16[1024,1024]{1,0:T(8,128)(2,1)} %collective-permute-done.7.other_ref), custom_call_target="tpu_custom_call" | custom-call | flops 1024 | bytes 1024 | tf_op jit(solution)/shard_map/align/pallas_call | solution.py:140
  106.7 1.8 %collective-permute-done.12.refs_3_ = bf16[256,1536]{1,0:T(8,128)(2,1)} collective-permute-done((bf16[256,1536]{1,0:T(8,128)(2,1)}, bf16[256,1536]{1,0:T(8,128)(2,1)}, u32[]{:S(2)}, u32[]{:S(2)}) %collective-permute-start.12) | collective-permute-done | bytes 786464 | tf_op jit(solution)/shard_map/ppermute | solution.py:292
  108.6 0.1 collective-permute-done.13.refs_4_
  108.7 12.0 %product.3.refs_4_ = f32[1024,4096]{1,0:T(8,128)} custom-call(s32[5]{0:T(128)} %stack.47.places.refs_0_, bf16[1024,2048]{1,0:T(8,128)(2,1)} %get-tuple-element.27.rows_ref.refs_1_, f32[1024,1]{1,0:T(8,128)} %get-tuple-element.28.sum_ref.refs_2_, bf16[512,1536]{1,0:T(8,128)(2,1)} %bitcast.5.refs_0_, bf16[512,1536]{1,0:T(8,128)(2,1)} %collective-permute-done.9.refs_1_, ...), custom_call_target="tpu_custom_call" | custom-call | flops 38654705664 | bytes 100663296 | tf_op jit(solution)/shard_map/product/pallas_call | solution.py:223
  120.7 20.5 %collective-permute-done.11.refs_4_ = bf16[512,1536]{1,0:T(8,128)(2,1)} collective-permute-done((bf16[512,1536]{1,0:T(8,128)(2,1)}, bf16[512,1536]{1,0:T(8,128)(2,1)}, u32[]{:S(2)}, u32[]{:S(2)}) %collective-permute-start.11) | collective-permute-done | bytes 1572896 | tf_op jit(solution)/shard_map/ppermute | solution.py:295
  141.1 0.2 collective-permute-done.10.refs_5_
  141.3 1.2 slice.15
  142.5 1.2 slice.14
  143.7 1.5 collective-permute-start.14
  145.3 2.0 %collective-permute-start.15 = (bf16[256,1536]{1,0:T(8,128)(2,1)S(1)}, bf16[256,1536]{1,0:T(8,128)(2,1)}, u32[]{:S(2)}, u32[]{:S(2)}) collective-permute-start(bf16[256,1536]{1,0:T(8,128)(2,1)S(1)} %slice.15), channel_id=1, source_target_pairs={{0,96},{1,97},{2,98},{3,99},{16,112},{17,113},{18,114},{19,115},{4... | collective-permute-start | bytes 2359304 | tf_op jit(solution)/shard_map/ppermute | solution.py:305
  147.2 8.3 %all-to-all-done.2.refs_3_ = bf16[32,4,16,1024]{3,2,1,0:T(8,128)(2,1)} async-done(((bf16[32,4,16,1024]{3,2,1,0:T(8,128)(2,1)}), bf16[32,4,16,1024]{3,2,1,0:T(8,128)(2,1)}, u32[]{:S(2)}, u32[]{:S(2)}) %all-to-all-start.2) | async-done | bytes 4194336 | tf_op jit(solution)/shard_map/all_to_all | solution.py:257
  155.5 9.1 %product.4.refs_8_ = f32[1024,4096]{1,0:T(8,128)} custom-call(s32[5]{0:T(128)} %stack.47.places.refs_0_, bf16[1024,2048]{1,0:T(8,128)(2,1)} %get-tuple-element.27.rows_ref.refs_1_, f32[1024,1]{1,0:T(8,128)} %get-tuple-element.28.sum_ref.refs_2_, bf16[32,4,16,1024]{3,2,1,0:T(8,128)(2,1)} %all-to-all-done.2.refs_3_, ...), custom_call_target="tpu_custom_call", output_to_operand_aliasing={{}: (4, {})} | custom-call | flops 25769803776 | bytes 75497472 | tf_op jit(solution)/shard_map/product/pallas_call | solution.py:223
  164.6 0.9 copy-done.7
  165.5 12.0 %product.5 = f32[1024,4096]{1,0:T(8,128)} custom-call(s32[5]{0:T(128)} %stack.47.places.refs_0_, bf16[1024,2048]{1,0:T(8,128)(2,1)} %get-tuple-element.27.rows_ref.refs_1_, f32[1024,1]{1,0:T(8,128)} %get-tuple-element.28.sum_ref.refs_2_, bf16[512,1536]{1,0:T(8,128)(2,1)} %bitcast.13.refs_3_, ...), custom_call_target="tpu_custom_call", output_to_operand_aliasing={{}: (8, {})} | custom-call | flops 38654705664 | bytes 100663296 | tf_op jit(solution)/shard_map/product/pallas_call | solution.py:223
  (22 shorter events, 0.1 us)
Async XLA Ops:
  2.4 37.9 %all-to-all-start = ((bf16[32,16,1536]{2,1,0:T(8,128)(2,1)}), bf16[32,16,1536]{2,1,0:T(8,128)(2,1)}, u32[]{:S(2)}, u32[]{:S(2)}) async-start(bf16[32,16,1536]{2,1,0:T(8,128)(2,1)} %pick.5), calls=%async_computation | async-start | bytes 3145728 | tf_op jit(solution)/shard_map/all_to_all | solution.py:257
  11.0 7.1 %copy-start.5 = (bf16[128,1024]{1,0:T(8,128)(2,1)S(1)}, bf16[128,1024]{1,0:T(8,128)(2,1)}, u32[]{:S(2)}) copy-start(bf16[128,1024]{1,0:T(8,128)(2,1)} %param.3) | copy-start | bytes 786436
  13.0 23.0 %collective-permute-start.2 = (bf16[16,16,1024]{2,1,0:T(8,128)(2,1)}, bf16[16,16,1024]{2,1,0:T(8,128)(2,1)S(1)}, u32[]{:S(2)}, u32[]{:S(2)}) collective-permute-start(bf16[16,16,1024]{2,1,0:T(8,128)(2,1)} %pick.4.refs_0_), channel_id=1, source_target_pairs={{0,64},{1,65},{2,66},{3,67},{16,80},{17,81},{18,82},{19,83},{4,68}... | collective-permute-start | bytes 1572872 | tf_op jit(solution)/shard_map/ppermute | solution.py:272
  16.1 24.1 %collective-permute-start.1 = (bf16[16,16,1024]{2,1,0:T(8,128)(2,1)}, bf16[16,16,1024]{2,1,0:T(8,128)(2,1)}, u32[]{:S(2)}, u32[]{:S(2)}) collective-permute-start(bf16[16,16,1024]{2,1,0:T(8,128)(2,1)} %pick.4.refs_0_), channel_id=1, source_target_pairs={{0,96},{1,97},{2,98},{3,99},{16,112},{17,113},{18,114},{19,115},{4... | collective-permute-start | bytes 1572872 | tf_op jit(solution)/shard_map/ppermute | solution.py:271
  17.3 23.0 %collective-permute-start = (bf16[16,16,1024]{2,1,0:T(8,128)(2,1)}, bf16[16,16,1024]{2,1,0:T(8,128)(2,1)}, u32[]{:S(2)}, u32[]{:S(2)}) collective-permute-start(bf16[16,16,1024]{2,1,0:T(8,128)(2,1)} %pick.4.refs_0_), channel_id=1, source_target_pairs={{0,32},{1,33},{2,34},{3,35},{16,48},{17,49},{18,50},{19,51},{4,36}... | collective-permute-start | bytes 1572872 | tf_op jit(solution)/shard_map/ppermute | solution.py:270
  18.2 17.9 %collective-permute-start.3 = (bf16[128,1024]{1,0:T(8,128)(2,1)S(1)}, bf16[128,1024]{1,0:T(8,128)(2,1)S(1)}, u32[]{:S(2)}, u32[]{:S(2)}) collective-permute-start(bf16[128,1024]{1,0:T(8,128)(2,1)S(1)} %copy-done.5), channel_id=1, source_target_pairs={{0,2},{1,3},{2,0},{3,1},{16,18},{17,19},{18,16},{19,17},{4,6},{5,7... | collective-permute-start | bytes 786440 | tf_op jit(solution)/shard_map/ppermute | solution.py:273
  36.0 11.1 %copy-start.1 = (bf16[16,16,1024]{2,1,0:T(8,128)(2,1)}, bf16[16,16,1024]{2,1,0:T(8,128)(2,1)S(1)}, u32[]{:S(2)}) copy-start(bf16[16,16,1024]{2,1,0:T(8,128)(2,1)S(1)} %collective-permute-done.2.refs_2_) | copy-start | bytes 1572868
  40.4 16.4 %collective-permute-start.5 = (bf16[2,128,1024]{2,1,0:T(8,128)(2,1)S(1)}, bf16[2,128,1024]{2,1,0:T(8,128)(2,1)S(1)}, u32[]{:S(2)}, u32[]{:S(2)}) collective-permute-start(bf16[2,128,1024]{2,1,0:T(8,128)(2,1)S(1)} %get-tuple-element.46), channel_id=1, source_target_pairs={{0,8},{1,9},{2,10},{3,11},{16,24},{17,25},{18,26},{19,27},{4,12},{... | collective-permute-start | bytes 1572872 | tf_op jit(solution)/shard_map/ppermute | solution.py:285
  42.5 24.5 %collective-permute-start.4 = (bf16[2,128,1024]{2,1,0:T(8,128)(2,1)S(1)}, bf16[2,128,1024]{2,1,0:T(8,128)(2,1)S(1)}, u32[]{:S(2)}, u32[]{:S(2)}) collective-permute-start(bf16[2,128,1024]{2,1,0:T(8,128)(2,1)S(1)} %get-tuple-element.46), channel_id=1, source_target_pairs={{0,12},{1,13},{2,14},{3,15},{16,28},{17,29},{18,30},{19,31},{4,0},... | collective-permute-start | bytes 1572872 | tf_op jit(solution)/shard_map/ppermute | solution.py:284
  44.0 24.1 %collective-permute-start.6 = (bf16[2,128,1024]{2,1,0:T(8,128)(2,1)S(1)}, bf16[2,128,1024]{2,1,0:T(8,128)(2,1)S(1)}, u32[]{:S(2)}, u32[]{:S(2)}) collective-permute-start(bf16[2,128,1024]{2,1,0:T(8,128)(2,1)S(1)} %get-tuple-element.46), channel_id=1, source_target_pairs={{0,4},{1,5},{2,6},{3,7},{16,20},{17,21},{18,22},{19,23},{4,8},{5,9... | collective-permute-start | bytes 1572872 | tf_op jit(solution)/shard_map/ppermute | solution.py:283
  44.5 35.9 %collective-permute-start.9 = (bf16[512,1536]{1,0:T(8,128)(2,1)}, bf16[512,1536]{1,0:T(8,128)(2,1)}, u32[]{:S(2)}, u32[]{:S(2)}) collective-permute-start(bf16[512,1536]{1,0:T(8,128)(2,1)} %bitcast.5.refs_0_), channel_id=1, source_target_pairs={{0,96},{1,97},{2,98},{3,99},{16,112},{17,113},{18,114},{19,115},{4... | collective-permute-start | bytes 4718600 | tf_op jit(solution)/shard_map/ppermute | solution.py:281
  47.2 36.7 %collective-permute-start.8 = (bf16[512,1536]{1,0:T(8,128)(2,1)}, bf16[512,1536]{1,0:T(8,128)(2,1)}, u32[]{:S(2)}, u32[]{:S(2)}) collective-permute-start(bf16[512,1536]{1,0:T(8,128)(2,1)} %bitcast.5.refs_0_), channel_id=1, source_target_pairs={{0,32},{1,33},{2,34},{3,35},{16,48},{17,49},{18,50},{19,51},{4,36}... | collective-permute-start | bytes 4718600 | tf_op jit(solution)/shard_map/ppermute | solution.py:280
  47.2 39.5 %all-to-all-start.1 = ((bf16[32,16,1536]{2,1,0:T(8,128)(2,1)}), bf16[32,16,1536]{2,1,0:T(8,128)(2,1)}, u32[]{:S(2)}, u32[]{:S(2)}) async-start(bf16[32,16,1536]{2,1,0:T(8,128)(2,1)} %pick.3), calls=%async_computation.1 | async-start | bytes 3145728 | tf_op jit(solution)/shard_map/all_to_all | solution.py:257
  56.8 11.2 %copy-start.2 = (bf16[2,128,1024]{2,1,0:T(8,128)(2,1)}, bf16[2,128,1024]{2,1,0:T(8,128)(2,1)S(1)}, u32[]{:S(2)}) copy-start(bf16[2,128,1024]{2,1,0:T(8,128)(2,1)S(1)} %collective-permute-done.5) | copy-start | bytes 1572868
  67.0 1.1 copy-start.3
  68.0 0.8 copy-start.4
  70.4 4.3 %copy-start = (bf16[4,2,128,1024]{3,2,1,0:T(8,128)(2,1)}, bf16[4,2,128,1024]{3,2,1,0:T(8,128)(2,1)S(1)}, u32[]{:S(2)}) copy-start(bf16[4,2,128,1024]{3,2,1,0:T(8,128)(2,1)S(1)} %pad_maximum_fusion) | copy-start | bytes 6291460
  70.5 29.9 %collective-permute-start.7 = (bf16[1024,1024]{1,0:T(8,128)(2,1)S(1)}, bf16[1024,1024]{1,0:T(8,128)(2,1)}, u32[]{:S(2)}, u32[]{:S(2)}) collective-permute-start(bf16[1024,1024]{1,0:T(8,128)(2,1)S(1)} %bitcast.15), channel_id=1, source_target_pairs={{0,1},{1,0},{2,3},{3,2},{16,17},{17,16},{18,19},{19,18},{4,5},{5,4... | collective-permute-start | bytes 6291464 | tf_op jit(solution)/shard_map/ppermute | solution.py:297
  86.6 11.1 %copy-start.6 = (s32[128]{0:T(128)S(1)}, s32[128]{0:T(128)}, u32[]{:S(2)}) copy-start(s32[128]{0:T(128)} %param.5) | copy-start | bytes 1540
  86.6 21.9 %collective-permute-start.12 = (bf16[256,1536]{1,0:T(8,128)(2,1)}, bf16[256,1536]{1,0:T(8,128)(2,1)}, u32[]{:S(2)}, u32[]{:S(2)}) collective-permute-start(bf16[256,1536]{1,0:T(8,128)(2,1)} %slice.16), channel_id=1, source_target_pairs={{0,32},{1,33},{2,34},{3,35},{16,48},{17,49},{18,50},{19,51},{4,36}... | collective-permute-start | bytes 2359304 | tf_op jit(solution)/shard_map/ppermute | solution.py:292
  88.1 20.5 %collective-permute-start.13 = (bf16[256,1536]{1,0:T(8,128)(2,1)S(1)}, bf16[256,1536]{1,0:T(8,128)(2,1)}, u32[]{:S(2)}, u32[]{:S(2)}) collective-permute-start(bf16[256,1536]{1,0:T(8,128)(2,1)S(1)} %slice.17), channel_id=1, source_target_pairs={{0,96},{1,97},{2,98},{3,99},{16,112},{17,113},{18,114},{19,115},{4... | collective-permute-start | bytes 2359304 | tf_op jit(solution)/shard_map/ppermute | solution.py:293
  89.9 65.7 %all-to-all-start.2 = ((bf16[32,4,16,1024]{3,2,1,0:T(8,128)(2,1)}), bf16[32,4,16,1024]{3,2,1,0:T(8,128)(2,1)}, u32[]{:S(2)}, u32[]{:S(2)}) async-start(bf16[32,4,16,1024]{3,2,1,0:T(8,128)(2,1)} %join.1), calls=%async_computation.2 | async-start | bytes 8388608 | tf_op jit(solution)/shard_map/all_to_all | solution.py:257
  98.3 42.8 %collective-permute-start.11 = (bf16[512,1536]{1,0:T(8,128)(2,1)}, bf16[512,1536]{1,0:T(8,128)(2,1)}, u32[]{:S(2)}, u32[]{:S(2)}) collective-permute-start(bf16[512,1536]{1,0:T(8,128)(2,1)} %bitcast.13.refs_3_), channel_id=1, source_target_pairs={{0,96},{1,97},{2,98},{3,99},{16,112},{17,113},{18,114},{19,115},{4... | collective-permute-start | bytes 4718600 | tf_op jit(solution)/shard_map/ppermute | solution.py:295
  98.6 42.7 %collective-permute-start.10 = (bf16[512,1536]{1,0:T(8,128)(2,1)}, bf16[512,1536]{1,0:T(8,128)(2,1)}, u32[]{:S(2)}, u32[]{:S(2)}) collective-permute-start(bf16[512,1536]{1,0:T(8,128)(2,1)} %bitcast.13.refs_3_), channel_id=1, source_target_pairs={{0,32},{1,33},{2,34},{3,35},{16,48},{17,49},{18,50},{19,51},{4,36}... | collective-permute-start | bytes 4718600 | tf_op jit(solution)/shard_map/ppermute | solution.py:294
  143.7 20.9 %collective-permute-start.14 = (bf16[256,1536]{1,0:T(8,128)(2,1)S(1)}, bf16[256,1536]{1,0:T(8,128)(2,1)S(1)}, u32[]{:S(2)}, u32[]{:S(2)}) collective-permute-start(bf16[256,1536]{1,0:T(8,128)(2,1)S(1)} %slice.14), channel_id=1, source_target_pairs={{0,32},{1,33},{2,34},{3,35},{16,48},{17,49},{18,50},{19,51},{4,36}... | collective-permute-start | bytes 2359304 | tf_op jit(solution)/shard_map/ppermute | solution.py:304
  145.3 19.4 %collective-permute-start.15 = (bf16[256,1536]{1,0:T(8,128)(2,1)S(1)}, bf16[256,1536]{1,0:T(8,128)(2,1)}, u32[]{:S(2)}, u32[]{:S(2)}) collective-permute-start(bf16[256,1536]{1,0:T(8,128)(2,1)S(1)} %slice.15), channel_id=1, source_target_pairs={{0,96},{1,97},{2,98},{3,99},{16,112},{17,113},{18,114},{19,115},{4... | collective-permute-start | bytes 2359304 | tf_op jit(solution)/shard_map/ppermute | solution.py:305
  164.6 0.9 copy-start.7

commit v4 on v3

--- a/solution.py
+++ b/solution.py
@@ -10,7 +10,7 @@
 AXES = ("row", "col")
 NX, NY, NZ, NC = 4, 4, 4, 2
 NCOL = NY * 2 * NC
-TILE = 512
+TILE = 256
 BLOCK = 256
 WEIGHT = 6
 WIDTHS = (1024, 1536, 1536)

time: 178 us -> 179 us (level)
  transfers between devices with their start and end apart: 19 -> 19, of which waited for: 13 -> 13; matrix products, arithmetic and copies ran while one was open for 5% -> 5% of each run, Pallas kernels for 20% -> 21%
where the time goes in v4:
time: 179 us; the launch traced here: 178 us
  waiting for transfers between devices  70.6 us (39%)
  Pallas kernels  51.4 us (29%)
  starting transfers between devices  45.5 us (25%)
  local copies, waits for them, and re-layouts  7.98 us (4%)
  other arithmetic  2.29 us (1%)
    pallas_call x3, Pallas kernels, product(): pl.pallas_call(kernel, out_shape=jax.ShapeDtypeStruct((comps, columns), j...  34 us
    all_to_all x3, starting transfers between devices, exchange(): lax.all_to_all(sent, AXES, 0, 0, tiled=True, axis_index_groups=SAME_X)  23.4 us
    ppermute x1, waiting for transfers between devices, body(): right_b = lax.ppermute(gotb, AXES, X_DOWN)  20 us
    ppermute x1, waiting for transfers between devices, body(): pair = lax.ppermute(increments, AXES, Z_PAIR)  14 us
    ppermute x1, waiting for transfers between devices, body(): above = lax.ppermute(near, AXES, Y_DOWN)  10.2 us
    all_to_all x3, waiting for transfers between devices, exchange(): lax.all_to_all(sent, AXES, 0, 0, tiled=True, axis_index_groups=SAME_X)  9.17 us
    pallas_call x3, Pallas kernels, pick(): pl.pallas_call(functools.partial(pick_kernel, offset), out_shape=jax.Shap...  6.83 us
    pallas_call x1, Pallas kernels, align(): pl.pallas_call(align_kernel, out_shape=(jax.ShapeDtypeStruct((comps, date...  6.35 us
  transfers between devices with their start and end apart: 19, of which 13 were waited for; matrix products, arithmetic and copies ran while one was open for 5% of the time, Pallas kernels for 21%

profile of v4, /device:TPU:8, one launch (start us, length us, event | category | flops | bytes accessed | tf_op | source)
XLA Modules:
  0.0 178.0 jit_solution(14586932638971377254)
XLA Ops:
  0.0 2.4 %pick.5 = bf16[32,16,1536]{2,1,0:T(8,128)(2,1)} custom-call(bf16[16,65536]{1,0:T(8,128)(2,1)} %states_ref.5), custom_call_target="tpu_custom_call" | custom-call | flops 1536 | bytes 1536 | tf_op jit(solution)/shard_map/pick/pallas_call | solution.py:70
  2.4 8.6 %all-to-all-start = ((bf16[32,16,1536]{2,1,0:T(8,128)(2,1)}), bf16[32,16,1536]{2,1,0:T(8,128)(2,1)}, u32[]{:S(2)}, u32[]{:S(2)}) async-start(bf16[32,16,1536]{2,1,0:T(8,128)(2,1)} %pick.5), calls=%async_computation | async-start | bytes 3145728 | tf_op jit(solution)/shard_map/all_to_all | solution.py:257
  11.0 2.0 %pick.4.refs_0_ = bf16[16,16,1024]{2,1,0:T(8,128)(2,1)} custom-call(bf16[16,65536]{1,0:T(8,128)(2,1)} %states_ref.5), custom_call_target="tpu_custom_call" | custom-call | flops 1024 | bytes 1024 | tf_op jit(solution)/shard_map/pick/pallas_call | solution.py:70
  13.0 3.1 %collective-permute-start.2 = (bf16[16,16,1024]{2,1,0:T(8,128)(2,1)}, bf16[16,16,1024]{2,1,0:T(8,128)(2,1)S(1)}, u32[]{:S(2)}, u32[]{:S(2)}) collective-permute-start(bf16[16,16,1024]{2,1,0:T(8,128)(2,1)} %pick.4.refs_0_), channel_id=1, source_target_pairs={{0,64},{1,65},{2,66},{3,67},{16,80},{17,81},{18,82},{19,83},{4,68}... | collective-permute-start | bytes 1572872 | tf_op jit(solution)/shard_map/ppermute | solution.py:272
  16.1 1.1 collective-permute-start.1
  17.3 0.9 collective-permute-start
  18.2 1.5 collective-permute-start.3
  19.6 2.4 %pick.3 = bf16[32,16,1536]{2,1,0:T(8,128)(2,1)} custom-call(bf16[16,65536]{1,0:T(8,128)(2,1)} %states_ref.5), custom_call_target="tpu_custom_call" | custom-call | flops 1536 | bytes 1536 | tf_op jit(solution)/shard_map/pick/pallas_call | solution.py:70
  22.1 14.0 %collective-permute-done.3 = bf16[128,1024]{1,0:T(8,128)(2,1)S(1)} collective-permute-done((bf16[128,1024]{1,0:T(8,128)(2,1)S(1)}, bf16[128,1024]{1,0:T(8,128)(2,1)S(1)}, u32[]{:S(2)}, u32[]{:S(2)}) %collective-permute-start.3) | collective-permute-done | bytes 262176 | tf_op jit(solution)/shard_map/ppermute | solution.py:273
  36.1 4.2 %collective-permute-done.1.refs_1_ = bf16[16,16,1024]{2,1,0:T(8,128)(2,1)} collective-permute-done((bf16[16,16,1024]{2,1,0:T(8,128)(2,1)}, bf16[16,16,1024]{2,1,0:T(8,128)(2,1)}, u32[]{:S(2)}, u32[]{:S(2)}) %collective-permute-start.1) | collective-permute-done | bytes 524320 | tf_op jit(solution)/shard_map/ppermute | solution.py:271
  40.4 2.2 %collective-permute-start.5 = (bf16[2,128,1024]{2,1,0:T(8,128)(2,1)S(1)}, bf16[2,128,1024]{2,1,0:T(8,128)(2,1)S(1)}, u32[]{:S(2)}, u32[]{:S(2)}) collective-permute-start(bf16[2,128,1024]{2,1,0:T(8,128)(2,1)S(1)} %get-tuple-element.46), channel_id=1, source_target_pairs={{0,8},{1,9},{2,10},{3,11},{16,24},{17,25},{18,26},{19,27},{4,12},{... | collective-permute-start | bytes 1572872 | tf_op jit(solution)/shard_map/ppermute | solution.py:285
  42.5 1.5 collective-permute-start.4
  44.0 0.6 collective-permute-start.6
  44.5 2.6 %collective-permute-start.9 = (bf16[512,1536]{1,0:T(8,128)(2,1)}, bf16[512,1536]{1,0:T(8,128)(2,1)}, u32[]{:S(2)}, u32[]{:S(2)}) collective-permute-start(bf16[512,1536]{1,0:T(8,128)(2,1)} %bitcast.5.refs_0_), channel_id=1, source_target_pairs={{0,96},{1,97},{2,98},{3,99},{16,112},{17,113},{18,114},{19,115},{4... | collective-permute-start | bytes 4718600 | tf_op jit(solution)/shard_map/ppermute | solution.py:281
  47.2 7.7 %all-to-all-start.1 = ((bf16[32,16,1536]{2,1,0:T(8,128)(2,1)}), bf16[32,16,1536]{2,1,0:T(8,128)(2,1)}, u32[]{:S(2)}, u32[]{:S(2)}) async-start(bf16[32,16,1536]{2,1,0:T(8,128)(2,1)} %pick.3), calls=%async_computation.1 | async-start | bytes 3145728 | tf_op jit(solution)/shard_map/all_to_all | solution.py:257
  54.9 1.9 %collective-permute-done.5 = bf16[2,128,1024]{2,1,0:T(8,128)(2,1)S(1)} collective-permute-done((bf16[2,128,1024]{2,1,0:T(8,128)(2,1)S(1)}, bf16[2,128,1024]{2,1,0:T(8,128)(2,1)S(1)}, u32[]{:S(2)}, u32[]{:S(2)}) %collective-permute-start.5) | collective-permute-done | bytes 524320 | tf_op jit(solution)/shard_map/ppermute | solution.py:285
  56.8 10.2 %collective-permute-done.4 = bf16[2,128,1024]{2,1,0:T(8,128)(2,1)S(1)} collective-permute-done((bf16[2,128,1024]{2,1,0:T(8,128)(2,1)S(1)}, bf16[2,128,1024]{2,1,0:T(8,128)(2,1)S(1)}, u32[]{:S(2)}, u32[]{:S(2)}) %collective-permute-start.4) | collective-permute-done | bytes 524320 | tf_op jit(solution)/shard_map/ppermute | solution.py:284
  67.0 1.0 collective-permute-done.6
  68.0 0.8 copy-done.4
  68.8 1.6 pad_maximum_fusion
  70.5 0.1 collective-permute-start.7
  70.6 4.2 %join.1 = bf16[32,4,16,1024]{3,2,1,0:T(8,128)(2,1)} custom-call(bf16[16,16,1024]{2,1,0:T(8,128)(2,1)} %pick.4.refs_0_, bf16[16,16,1024]{2,1,0:T(8,128)(2,1)} %collective-permute-done.1.refs_1_, bf16[16,16,1024]{2,1,0:T(8,128)(2,1)} %copy-done.1, bf16[16,16,1024]{2,1,0:T(8,128)(2,1)} %collective-permute-done.refs_3_), custom_call_target="tpu_custom_call" | custom-call | flops 1024 | bytes 1024 | tf_op jit(solution)/shard_map/join/pallas_call | solution.py:91
  74.8 5.7 %collective-permute-done.9.refs_1_ = bf16[512,1536]{1,0:T(8,128)(2,1)} collective-permute-done((bf16[512,1536]{1,0:T(8,128)(2,1)}, bf16[512,1536]{1,0:T(8,128)(2,1)}, u32[]{:S(2)}, u32[]{:S(2)}) %collective-permute-start.9) | collective-permute-done | bytes 1572896 | tf_op jit(solution)/shard_map/ppermute | solution.py:281
  80.5 1.2 slice.17
  81.7 2.2 %collective-permute-done.8.refs_2_ = bf16[512,1536]{1,0:T(8,128)(2,1)} collective-permute-done((bf16[512,1536]{1,0:T(8,128)(2,1)}, bf16[512,1536]{1,0:T(8,128)(2,1)}, u32[]{:S(2)}, u32[]{:S(2)}) %collective-permute-start.8) | collective-permute-done | bytes 1572896 | tf_op jit(solution)/shard_map/ppermute | solution.py:280
  83.9 2.1 %slice.16 = bf16[256,1536]{1,0:T(8,128)(2,1)} slice(bf16[512,1536]{1,0:T(8,128)(2,1)} %collective-permute-done.8.refs_2_), slice={[0:256], [0:1536]} | slice | bytes 1572864 | tf_op jit(solution)/shard_map/slice | solution.py:290
  86.0 0.7 all-to-all-done.1
  86.6 1.5 collective-permute-start.12
  88.1 1.7 collective-permute-start.13
  89.9 7.1 %all-to-all-start.2 = ((bf16[32,4,16,1024]{3,2,1,0:T(8,128)(2,1)}), bf16[32,4,16,1024]{3,2,1,0:T(8,128)(2,1)}, u32[]{:S(2)}, u32[]{:S(2)}) async-start(bf16[32,4,16,1024]{3,2,1,0:T(8,128)(2,1)} %join.1), calls=%async_computation.2 | async-start | bytes 8388608 | tf_op jit(solution)/shard_map/all_to_all | solution.py:257
  97.1 0.7 stack.47.places.refs_0_
  97.7 0.6 fusion.10.starts
  98.3 0.3 collective-permute-start.11
  98.6 1.8 collective-permute-start.10
  100.4 6.4 %align.1 = (bf16[1024,2048]{1,0:T(8,128)(2,1)}, f32[1024,1]{1,0:T(8,128)}) custom-call(s32[128]{0:T(128)} %fusion.10.starts, bf16[1024,1024]{1,0:T(8,128)(2,1)} %bitcast.16, bf16[1024,1024]{1,0:T(8,128)(2,1)} %collective-permute-done.7.other_ref), custom_call_target="tpu_custom_call" | custom-call | flops 1024 | bytes 1024 | tf_op jit(solution)/shard_map/align/pallas_call | solution.py:140
  106.7 1.8 %collective-permute-done.12.refs_3_ = bf16[256,1536]{1,0:T(8,128)(2,1)} collective-permute-done((bf16[256,1536]{1,0:T(8,128)(2,1)}, bf16[256,1536]{1,0:T(8,128)(2,1)}, u32[]{:S(2)}, u32[]{:S(2)}) %collective-permute-start.12) | collective-permute-done | bytes 786464 | tf_op jit(solution)/shard_map/ppermute | solution.py:292
  108.6 0.1 collective-permute-done.13.refs_4_
  108.7 12.4 %product.3.refs_4_ = f32[1024,4096]{1,0:T(8,128)} custom-call(s32[5]{0:T(128)} %stack.47.places.refs_0_, bf16[1024,2048]{1,0:T(8,128)(2,1)} %get-tuple-element.27.rows_ref.refs_1_, f32[1024,1]{1,0:T(8,128)} %get-tuple-element.28.sum_ref.refs_2_, bf16[512,1536]{1,0:T(8,128)(2,1)} %bitcast.5.refs_0_, bf16[512,1536]{1,0:T(8,128)(2,1)} %collective-permute-done.9.refs_1_, ...), custom_call_target="tpu_custom_call" | custom-call | flops 38654705664 | bytes 100663296 | tf_op jit(solution)/shard_map/product/pallas_call | solution.py:223
  121.1 20.0 %collective-permute-done.11.refs_4_ = bf16[512,1536]{1,0:T(8,128)(2,1)} collective-permute-done((bf16[512,1536]{1,0:T(8,128)(2,1)}, bf16[512,1536]{1,0:T(8,128)(2,1)}, u32[]{:S(2)}, u32[]{:S(2)}) %collective-permute-start.11) | collective-permute-done | bytes 1572896 | tf_op jit(solution)/shard_map/ppermute | solution.py:295
  141.1 0.2 collective-permute-done.10.refs_5_
  141.3 1.2 slice.15
  142.5 1.2 slice.14
  143.7 1.4 collective-permute-start.14
  145.1 2.0 %collective-permute-start.15 = (bf16[256,1536]{1,0:T(8,128)(2,1)S(1)}, bf16[256,1536]{1,0:T(8,128)(2,1)}, u32[]{:S(2)}, u32[]{:S(2)}) collective-permute-start(bf16[256,1536]{1,0:T(8,128)(2,1)S(1)} %slice.15), channel_id=1, source_target_pairs={{0,96},{1,97},{2,98},{3,99},{16,112},{17,113},{18,114},{19,115},{4... | collective-permute-start | bytes 2359304 | tf_op jit(solution)/shard_map/ppermute | solution.py:305
  147.0 8.5 %all-to-all-done.2.refs_3_ = bf16[32,4,16,1024]{3,2,1,0:T(8,128)(2,1)} async-done(((bf16[32,4,16,1024]{3,2,1,0:T(8,128)(2,1)}), bf16[32,4,16,1024]{3,2,1,0:T(8,128)(2,1)}, u32[]{:S(2)}, u32[]{:S(2)}) %all-to-all-start.2) | async-done | bytes 4194336 | tf_op jit(solution)/shard_map/all_to_all | solution.py:257
  155.5 9.2 %product.4.refs_8_ = f32[1024,4096]{1,0:T(8,128)} custom-call(s32[5]{0:T(128)} %stack.47.places.refs_0_, bf16[1024,2048]{1,0:T(8,128)(2,1)} %get-tuple-element.27.rows_ref.refs_1_, f32[1024,1]{1,0:T(8,128)} %get-tuple-element.28.sum_ref.refs_2_, bf16[32,4,16,1024]{3,2,1,0:T(8,128)(2,1)} %all-to-all-done.2.refs_3_, ...), custom_call_target="tpu_custom_call", output_to_operand_aliasing={{}: (4, {})} | custom-call | flops 25769803776 | bytes 75497472 | tf_op jit(solution)/shard_map/product/pallas_call | solution.py:223
  164.8 0.9 copy-done.7
  165.6 12.4 %product.5 = f32[1024,4096]{1,0:T(8,128)} custom-call(s32[5]{0:T(128)} %stack.47.places.refs_0_, bf16[1024,2048]{1,0:T(8,128)(2,1)} %get-tuple-element.27.rows_ref.refs_1_, f32[1024,1]{1,0:T(8,128)} %get-tuple-element.28.sum_ref.refs_2_, bf16[512,1536]{1,0:T(8,128)(2,1)} %bitcast.13.refs_3_, ...), custom_call_target="tpu_custom_call", output_to_operand_aliasing={{}: (8, {})} | custom-call | flops 38654705664 | bytes 100663296 | tf_op jit(solution)/shard_map/product/pallas_call | solution.py:223
  (22 shorter events, 0.1 us)
Async XLA Ops:
  2.4 37.9 %all-to-all-start = ((bf16[32,16,1536]{2,1,0:T(8,128)(2,1)}), bf16[32,16,1536]{2,1,0:T(8,128)(2,1)}, u32[]{:S(2)}, u32[]{:S(2)}) async-start(bf16[32,16,1536]{2,1,0:T(8,128)(2,1)} %pick.5), calls=%async_computation | async-start | bytes 3145728 | tf_op jit(solution)/shard_map/all_to_all | solution.py:257
  11.0 7.1 %copy-start.5 = (bf16[128,1024]{1,0:T(8,128)(2,1)S(1)}, bf16[128,1024]{1,0:T(8,128)(2,1)}, u32[]{:S(2)}) copy-start(bf16[128,1024]{1,0:T(8,128)(2,1)} %param.3) | copy-start | bytes 786436
  13.0 23.0 %collective-permute-start.2 = (bf16[16,16,1024]{2,1,0:T(8,128)(2,1)}, bf16[16,16,1024]{2,1,0:T(8,128)(2,1)S(1)}, u32[]{:S(2)}, u32[]{:S(2)}) collective-permute-start(bf16[16,16,1024]{2,1,0:T(8,128)(2,1)} %pick.4.refs_0_), channel_id=1, source_target_pairs={{0,64},{1,65},{2,66},{3,67},{16,80},{17,81},{18,82},{19,83},{4,68}... | collective-permute-start | bytes 1572872 | tf_op jit(solution)/shard_map/ppermute | solution.py:272
  16.1 24.1 %collective-permute-start.1 = (bf16[16,16,1024]{2,1,0:T(8,128)(2,1)}, bf16[16,16,1024]{2,1,0:T(8,128)(2,1)}, u32[]{:S(2)}, u32[]{:S(2)}) collective-permute-start(bf16[16,16,1024]{2,1,0:T(8,128)(2,1)} %pick.4.refs_0_), channel_id=1, source_target_pairs={{0,96},{1,97},{2,98},{3,99},{16,112},{17,113},{18,114},{19,115},{4... | collective-permute-start | bytes 1572872 | tf_op jit(solution)/shard_map/ppermute | solution.py:271
  17.3 23.0 %collective-permute-start = (bf16[16,16,1024]{2,1,0:T(8,128)(2,1)}, bf16[16,16,1024]{2,1,0:T(8,128)(2,1)}, u32[]{:S(2)}, u32[]{:S(2)}) collective-permute-start(bf16[16,16,1024]{2,1,0:T(8,128)(2,1)} %pick.4.refs_0_), channel_id=1, source_target_pairs={{0,32},{1,33},{2,34},{3,35},{16,48},{17,49},{18,50},{19,51},{4,36}... | collective-permute-start | bytes 1572872 | tf_op jit(solution)/shard_map/ppermute | solution.py:270
  18.2 17.9 %collective-permute-start.3 = (bf16[128,1024]{1,0:T(8,128)(2,1)S(1)}, bf16[128,1024]{1,0:T(8,128)(2,1)S(1)}, u32[]{:S(2)}, u32[]{:S(2)}) collective-permute-start(bf16[128,1024]{1,0:T(8,128)(2,1)S(1)} %copy-done.5), channel_id=1, source_target_pairs={{0,2},{1,3},{2,0},{3,1},{16,18},{17,19},{18,16},{19,17},{4,6},{5,7... | collective-permute-start | bytes 786440 | tf_op jit(solution)/shard_map/ppermute | solution.py:273
  36.0 11.1 %copy-start.1 = (bf16[16,16,1024]{2,1,0:T(8,128)(2,1)}, bf16[16,16,1024]{2,1,0:T(8,128)(2,1)S(1)}, u32[]{:S(2)}) copy-start(bf16[16,16,1024]{2,1,0:T(8,128)(2,1)S(1)} %collective-permute-done.2.refs_2_) | copy-start | bytes 1572868
  40.4 16.4 %collective-permute-start.5 = (bf16[2,128,1024]{2,1,0:T(8,128)(2,1)S(1)}, bf16[2,128,1024]{2,1,0:T(8,128)(2,1)S(1)}, u32[]{:S(2)}, u32[]{:S(2)}) collective-permute-start(bf16[2,128,1024]{2,1,0:T(8,128)(2,1)S(1)} %get-tuple-element.46), channel_id=1, source_target_pairs={{0,8},{1,9},{2,10},{3,11},{16,24},{17,25},{18,26},{19,27},{4,12},{... | collective-permute-start | bytes 1572872 | tf_op jit(solution)/shard_map/ppermute | solution.py:285
  42.5 24.5 %collective-permute-start.4 = (bf16[2,128,1024]{2,1,0:T(8,128)(2,1)S(1)}, bf16[2,128,1024]{2,1,0:T(8,128)(2,1)S(1)}, u32[]{:S(2)}, u32[]{:S(2)}) collective-permute-start(bf16[2,128,1024]{2,1,0:T(8,128)(2,1)S(1)} %get-tuple-element.46), channel_id=1, source_target_pairs={{0,12},{1,13},{2,14},{3,15},{16,28},{17,29},{18,30},{19,31},{4,0},... | collective-permute-start | bytes 1572872 | tf_op jit(solution)/shard_map/ppermute | solution.py:284
  44.0 24.1 %collective-permute-start.6 = (bf16[2,128,1024]{2,1,0:T(8,128)(2,1)S(1)}, bf16[2,128,1024]{2,1,0:T(8,128)(2,1)S(1)}, u32[]{:S(2)}, u32[]{:S(2)}) collective-permute-start(bf16[2,128,1024]{2,1,0:T(8,128)(2,1)S(1)} %get-tuple-element.46), channel_id=1, source_target_pairs={{0,4},{1,5},{2,6},{3,7},{16,20},{17,21},{18,22},{19,23},{4,8},{5,9... | collective-permute-start | bytes 1572872 | tf_op jit(solution)/shard_map/ppermute | solution.py:283
  44.5 35.9 %collective-permute-start.9 = (bf16[512,1536]{1,0:T(8,128)(2,1)}, bf16[512,1536]{1,0:T(8,128)(2,1)}, u32[]{:S(2)}, u32[]{:S(2)}) collective-permute-start(bf16[512,1536]{1,0:T(8,128)(2,1)} %bitcast.5.refs_0_), channel_id=1, source_target_pairs={{0,96},{1,97},{2,98},{3,99},{16,112},{17,113},{18,114},{19,115},{4... | collective-permute-start | bytes 4718600 | tf_op jit(solution)/shard_map/ppermute | solution.py:281
  47.2 36.7 %collective-permute-start.8 = (bf16[512,1536]{1,0:T(8,128)(2,1)}, bf16[512,1536]{1,0:T(8,128)(2,1)}, u32[]{:S(2)}, u32[]{:S(2)}) collective-permute-start(bf16[512,1536]{1,0:T(8,128)(2,1)} %bitcast.5.refs_0_), channel_id=1, source_target_pairs={{0,32},{1,33},{2,34},{3,35},{16,48},{17,49},{18,50},{19,51},{4,36}... | collective-permute-start | bytes 4718600 | tf_op jit(solution)/shard_map/ppermute | solution.py:280
  47.2 39.5 %all-to-all-start.1 = ((bf16[32,16,1536]{2,1,0:T(8,128)(2,1)}), bf16[32,16,1536]{2,1,0:T(8,128)(2,1)}, u32[]{:S(2)}, u32[]{:S(2)}) async-start(bf16[32,16,1536]{2,1,0:T(8,128)(2,1)} %pick.3), calls=%async_computation.1 | async-start | bytes 3145728 | tf_op jit(solution)/shard_map/all_to_all | solution.py:257
  56.8 11.2 %copy-start.2 = (bf16[2,128,1024]{2,1,0:T(8,128)(2,1)}, bf16[2,128,1024]{2,1,0:T(8,128)(2,1)S(1)}, u32[]{:S(2)}) copy-start(bf16[2,128,1024]{2,1,0:T(8,128)(2,1)S(1)} %collective-permute-done.5) | copy-start | bytes 1572868
  67.0 1.1 copy-start.3
  68.0 0.8 copy-start.4
  70.4 4.3 %copy-start = (bf16[4,2,128,1024]{3,2,1,0:T(8,128)(2,1)}, bf16[4,2,128,1024]{3,2,1,0:T(8,128)(2,1)S(1)}, u32[]{:S(2)}) copy-start(bf16[4,2,128,1024]{3,2,1,0:T(8,128)(2,1)S(1)} %pad_maximum_fusion) | copy-start | bytes 6291460
  70.5 29.9 %collective-permute-start.7 = (bf16[1024,1024]{1,0:T(8,128)(2,1)S(1)}, bf16[1024,1024]{1,0:T(8,128)(2,1)}, u32[]{:S(2)}, u32[]{:S(2)}) collective-permute-start(bf16[1024,1024]{1,0:T(8,128)(2,1)S(1)} %bitcast.15), channel_id=1, source_target_pairs={{0,1},{1,0},{2,3},{3,2},{16,17},{17,16},{18,19},{19,18},{4,5},{5,4... | collective-permute-start | bytes 6291464 | tf_op jit(solution)/shard_map/ppermute | solution.py:297
  86.6 11.1 %copy-start.6 = (s32[128]{0:T(128)S(1)}, s32[128]{0:T(128)}, u32[]{:S(2)}) copy-start(s32[128]{0:T(128)} %param.5) | copy-start | bytes 1540
  86.6 21.9 %collective-permute-start.12 = (bf16[256,1536]{1,0:T(8,128)(2,1)}, bf16[256,1536]{1,0:T(8,128)(2,1)}, u32[]{:S(2)}, u32[]{:S(2)}) collective-permute-start(bf16[256,1536]{1,0:T(8,128)(2,1)} %slice.16), channel_id=1, source_target_pairs={{0,32},{1,33},{2,34},{3,35},{16,48},{17,49},{18,50},{19,51},{4,36}... | collective-permute-start | bytes 2359304 | tf_op jit(solution)/shard_map/ppermute | solution.py:292
  88.1 20.5 %collective-permute-start.13 = (bf16[256,1536]{1,0:T(8,128)(2,1)S(1)}, bf16[256,1536]{1,0:T(8,128)(2,1)}, u32[]{:S(2)}, u32[]{:S(2)}) collective-permute-start(bf16[256,1536]{1,0:T(8,128)(2,1)S(1)} %slice.17), channel_id=1, source_target_pairs={{0,96},{1,97},{2,98},{3,99},{16,112},{17,113},{18,114},{19,115},{4... | collective-permute-start | bytes 2359304 | tf_op jit(solution)/shard_map/ppermute | solution.py:293
  89.9 65.7 %all-to-all-start.2 = ((bf16[32,4,16,1024]{3,2,1,0:T(8,128)(2,1)}), bf16[32,4,16,1024]{3,2,1,0:T(8,128)(2,1)}, u32[]{:S(2)}, u32[]{:S(2)}) async-start(bf16[32,4,16,1024]{3,2,1,0:T(8,128)(2,1)} %join.1), calls=%async_computation.2 | async-start | bytes 8388608 | tf_op jit(solution)/shard_map/all_to_all | solution.py:257
  98.3 42.8 %collective-permute-start.11 = (bf16[512,1536]{1,0:T(8,128)(2,1)}, bf16[512,1536]{1,0:T(8,128)(2,1)}, u32[]{:S(2)}, u32[]{:S(2)}) collective-permute-start(bf16[512,1536]{1,0:T(8,128)(2,1)} %bitcast.13.refs_3_), channel_id=1, source_target_pairs={{0,96},{1,97},{2,98},{3,99},{16,112},{17,113},{18,114},{19,115},{4... | collective-permute-start | bytes 4718600 | tf_op jit(solution)/shard_map/ppermute | solution.py:295
  98.6 42.7 %collective-permute-start.10 = (bf16[512,1536]{1,0:T(8,128)(2,1)}, bf16[512,1536]{1,0:T(8,128)(2,1)}, u32[]{:S(2)}, u32[]{:S(2)}) collective-permute-start(bf16[512,1536]{1,0:T(8,128)(2,1)} %bitcast.13.refs_3_), channel_id=1, source_target_pairs={{0,32},{1,33},{2,34},{3,35},{16,48},{17,49},{18,50},{19,51},{4,36}... | collective-permute-start | bytes 4718600 | tf_op jit(solution)/shard_map/ppermute | solution.py:294
  143.7 21.0 %collective-permute-start.14 = (bf16[256,1536]{1,0:T(8,128)(2,1)S(1)}, bf16[256,1536]{1,0:T(8,128)(2,1)S(1)}, u32[]{:S(2)}, u32[]{:S(2)}) collective-permute-start(bf16[256,1536]{1,0:T(8,128)(2,1)S(1)} %slice.14), channel_id=1, source_target_pairs={{0,32},{1,33},{2,34},{3,35},{16,48},{17,49},{18,50},{19,51},{4,36}... | collective-permute-start | bytes 2359304 | tf_op jit(solution)/shard_map/ppermute | solution.py:304
  145.1 19.7 %collective-permute-start.15 = (bf16[256,1536]{1,0:T(8,128)(2,1)S(1)}, bf16[256,1536]{1,0:T(8,128)(2,1)}, u32[]{:S(2)}, u32[]{:S(2)}) collective-permute-start(bf16[256,1536]{1,0:T(8,128)(2,1)S(1)} %slice.15), channel_id=1, source_target_pairs={{0,96},{1,97},{2,98},{3,99},{16,112},{17,113},{18,114},{19,115},{4... | collective-permute-start | bytes 2359304 | tf_op jit(solution)/shard_map/ppermute | solution.py:305
  164.7 0.9 copy-start.7
